TPU v7x, 32 devices: a whole 2x2x4 slice. The times are simulated.
32 devices in a mesh: leaf: 8 (over z, x), front: 4 (over y, core).
Axes of the slice: x: 2, y: 2, z: 4, core: 2. Of those that a mesh axis runs over, the one named last changes fastest.
Arguments:
- child_update: bfloat16 [8, 4, 1, 3, 256, 3072], P('leaf', 'front'), may hold values from -60 to 60, as said below
- sep_one: bfloat16 [8, 4, 1, 4, 256, 512], P('leaf', 'front'), may hold values from -60 to 60, as said below
- sep_two: bfloat16 [8, 4, 1, 4, 256, 256], P('leaf', 'front'), may hold values from -60 to 60, as said below
- map_one: int32 [8, 1, 4, 3], replicated, may hold values from 0 to 3, as said below
- map_two: int32 [4, 1, 4, 3], replicated, may hold values from 0 to 3, as said below
- mask_one: int32 [4, 1, 12, 4], replicated, may hold values 0 or 1
- mask_two: int32 [2, 1, 12, 4], replicated, may hold values 0 or 1
Outputs:
- factor_one: float32 [8, 4, 1, 4, 256, 512], P('leaf', 'front')
- factor_two: float32 [8, 4, 1, 4, 256, 256], P('leaf', 'front')
- update_two: bfloat16 [8, 4, 1, 3, 256, 768], P('leaf', 'front')
Inputs may be any that keep to these rules, and one draw needn't show every extreme that they name: `child_update`: every child[l,b] is symmetric positive definite. `sep_one`: the top 1024 rows of each front's initial entries form a symmetric positive definite block, and every assembled front is positive definite. `sep_two`: the top 1024 rows of each front's initial entries form a symmetric positive definite block, and every assembled front is positive definite. `map_one`: for each child, batch and j the 3 entries are distinct; the two children 2p and 2p + 1 leave out different slots, so every parent tile receives one or two child tiles. `map_two`: for each first-level front, batch and j the 3 entries are distinct; fronts 2q and 2q + 1 leave out different slots, so every parent tile receives one or two child tiles.
All inputs are finite; a program needn't handle non-finite values.
Results may differ from a plain program's by a relative error of at most 0.0047.
Values may be sent and summed in bfloat16 or wider, within the bound.
No kernel may reach another device: no remote copies, remote signals or barrier semaphores. Data moves between devices by JAX's collectives and lax.ppermute only.
A program may use at most 192 MiB of HBM per device.

v0:
```python
import jax
import jax.numpy as jnp
from jax import lax
from jax.sharding import PartitionSpec as P

TILE = 256
ST = 4
UT = 12
FT = 16
S = 1024
U = 3072
F = 4096


def swapped(value, axis, apart):
    mask = 2**apart
    pairs = [(source, source ^ mask) for source in range(lax.axis_size(axis))]
    return lax.ppermute(value, axis, pairs)


def place_tiles(blocks, row_source, row_live, col_source, col_live):
    taken = jnp.take(blocks, row_source, axis=0)
    taken = jnp.take(taken, col_source, axis=2)
    keep = jnp.logical_and(row_live[:, None, None, None], col_live[None, None, :, None])
    return jnp.where(keep, taken.astype(jnp.float32), 0.0)


def place_child(child_rows, tile_map, column):
    batch_count = child_rows.shape[0]
    local_tiles = child_rows.shape[1]
    groups = tile_map.shape[1]
    slot_count = FT // groups
    own_slots = lax.dynamic_index_in_dim(tile_map, column, 1, keepdims=False)
    row_hit = own_slots[..., None] == jnp.arange(slot_count, dtype=jnp.int32)
    row_source = jnp.sum(
        row_hit.astype(jnp.int32) * jnp.arange(local_tiles, dtype=jnp.int32)[None, :, None], axis=1
    )
    row_live = jnp.any(row_hit, axis=1)
    targets = (jnp.swapaxes(tile_map, 1, 2) * groups + jnp.arange(groups, dtype=jnp.int32)).reshape(
        batch_count, UT
    )
    col_hit = targets[..., None] == jnp.arange(FT, dtype=jnp.int32)
    col_source = jnp.sum(
        col_hit.astype(jnp.int32) * jnp.arange(UT, dtype=jnp.int32)[None, :, None], axis=1
    )
    col_live = jnp.any(col_hit, axis=1)
    blocks = child_rows.reshape(batch_count, local_tiles, TILE, UT, TILE)
    placed = jax.vmap(place_tiles)(blocks, row_source, row_live, col_source, col_live)
    return placed.reshape(batch_count, slot_count, TILE, F)


def join_halves(mine, other, position):
    lower_first = jnp.concatenate([mine, other], axis=-1)
    upper_first = jnp.concatenate([other, mine], axis=-1)
    return jnp.where(position == 0, lower_first, upper_first)


def add_initial(canvas, initial, mask_front, column):
    batch_count = canvas.shape[0]
    slot_count = canvas.shape[1]
    groups = lax.axis_size("front")
    mask_rows = mask_front.reshape(batch_count, slot_count - 1, groups, ST)
    mask_rows = lax.dynamic_index_in_dim(mask_rows, column, 2, keepdims=False).astype(jnp.float32)
    mask_all = jnp.concatenate([jnp.ones((batch_count, 1, ST), jnp.float32), mask_rows], axis=1)
    weighted = initial.astype(jnp.float32).reshape(batch_count, slot_count, TILE, ST, TILE)
    weighted = (weighted * mask_all[:, :, None, :, None]).reshape(batch_count, slot_count, TILE, S)
    return jnp.concatenate([canvas[:, :, :, :S] + weighted, canvas[:, :, :, S:]], axis=-1)


def factor_front(canvas, column):
    batch_count = canvas.shape[0]
    local_tiles = canvas.shape[1] - 1
    groups = lax.axis_size("front")
    pivot_piece = canvas[:, :1, :, :S]
    pivot_all = lax.all_gather(pivot_piece[None], "front", axis=0, tiled=True)
    pivot_block = jnp.moveaxis(pivot_all, 0, 2).reshape(batch_count, S, S)
    lower_factor = jnp.linalg.cholesky(pivot_block)
    coupling = canvas[:, 1:, :, :S].reshape(batch_count, local_tiles * TILE, S)
    panel_full = lax.linalg.triangular_solve(
        lower_factor, coupling, left_side=False, lower=True, transpose_a=True
    )
    panel_round = panel_full.astype(jnp.bfloat16)
    shared = lax.all_gather(
        panel_round.reshape(batch_count, local_tiles, TILE, S)[None], "front", axis=0, tiled=True
    )
    ordered = jnp.transpose(shared, (1, 2, 0, 3, 4)).reshape(batch_count, U, S)
    own_lower = lax.dynamic_index_in_dim(
        lower_factor.reshape(batch_count, groups, TILE, S), column, 1, keepdims=True
    )
    factor_rows = jnp.concatenate(
        [own_lower, panel_full.reshape(batch_count, local_tiles, TILE, S)], axis=1
    )
    trailing = canvas[:, 1:, :, S:].reshape(batch_count, local_tiles * TILE, U)
    product = jnp.einsum("brk,bnk->brn", panel_round, ordered, preferred_element_type=jnp.float32)
    update = (trailing - product).astype(jnp.bfloat16)
    return (factor_rows, update)


def body(child_update, sep_one, sep_two, map_one, map_two, mask_one, mask_two):
    column = lax.axis_index("front")
    leaf_index = lax.axis_index("leaf")
    half_index = leaf_index % 2
    quarter_index = leaf_index % 4
    pair_index = leaf_index // 2
    quad_index = leaf_index // 4
    side_index = pair_index % 2
    child_rows = child_update[0, 0]
    batch_count = child_rows.shape[0]
    local_tiles = child_rows.shape[1]
    entries_one = sep_one[0, 0]
    entries_two = sep_two[0, 0]
    peer_rows, peer_one, peer_two = swapped((child_rows, entries_one, entries_two), "leaf", 0)
    map_own = lax.dynamic_index_in_dim(map_one, leaf_index, 0, keepdims=False)
    map_peer = lax.dynamic_index_in_dim(map_one, jnp.bitwise_xor(leaf_index, 1), 0, keepdims=False)
    front_first = place_child(child_rows, map_own, column) + place_child(
        peer_rows, map_peer, column
    )
    initial_one = join_halves(entries_one, peer_one, half_index)
    mask_front = lax.dynamic_index_in_dim(mask_one, pair_index, 0, keepdims=False)
    front_first = add_initial(front_first, initial_one, mask_front, column)
    factor_rows_one, update_one = factor_front(front_first, column)
    factor_one = lax.dynamic_slice_in_dim(factor_rows_one, half_index * (S // 2), S // 2, 3)
    entries_half = join_halves(entries_two, peer_two, quarter_index % 2)
    update_far, entries_far = swapped((update_one, entries_half), "leaf", 1)
    map_near = lax.dynamic_index_in_dim(map_two, pair_index, 0, keepdims=False)
    map_far = lax.dynamic_index_in_dim(map_two, jnp.bitwise_xor(pair_index, 1), 0, keepdims=False)
    near_rows = update_one.reshape(batch_count, local_tiles, TILE, U)
    far_rows = update_far.reshape(batch_count, local_tiles, TILE, U)
    front_second = place_child(near_rows, map_near, column) + place_child(far_rows, map_far, column)
    initial_two = join_halves(entries_half, entries_far, side_index)
    mask_second = lax.dynamic_index_in_dim(mask_two, quad_index, 0, keepdims=False)
    front_second = add_initial(front_second, initial_two, mask_second, column)
    factor_rows_two, update_last = factor_front(front_second, column)
    update_last = lax.dynamic_slice_in_dim(update_last, quarter_index * (U // 4), U // 4, 2)
    factor_two = lax.dynamic_slice_in_dim(factor_rows_two, quarter_index * (S // 4), S // 4, 3)
    update_two = update_last.reshape(batch_count, local_tiles, TILE, U // 4)
    return (factor_one[None, None], factor_two[None, None], update_two[None, None])


def solution(mesh):
    return jax.shard_map(
        body,
        mesh=mesh,
        in_specs=(
            P("leaf", "front", None, None, None, None),
            P("leaf", "front", None, None, None, None),
            P("leaf", "front", None, None, None, None),
            P(),
            P(),
            P(),
            P(),
        ),
        out_specs=(
            P("leaf", "front", None, None, None, None),
            P("leaf", "front", None, None, None, None),
            P("leaf", "front", None, None, None, None),
        ),
        check_vma=False,
    )
```

profile of v0, /device:TPU:0, one launch (start us, length us, event | category | flops | bytes accessed | tf_op | source)
XLA Modules:
  0.0 1310.3 jit_solution(10803977760372575145)
XLA Ops:
  47.4 88.7 %collective-permute-done = bf16[1,3,256,3072]{2,3,1,0:T(8,128)(2,1)} collective-permute-done((bf16[1,3,256,3072]{2,3,1,0:T(8,128)(2,1)}, bf16[1,3,256,3072]{2,3,1,0:T(8,128)(2,1)}, u32[]{:S(2)}, u32[]{:S(2)}) %collective-permute-start) | collective-permute-done | bytes 4718624 | tf_op jit(solution)/shard_map/ppermute | solution.py:18
  162.4 13.8 %select_add_fusion.1 = f32[1,4,256,16,256]{4,2,1,3,0:T(8,128)} fusion(bf16[16,4,256,256]{3,2,1,0:T(8,128)(2,1)} %gather_fusion.3, bf16[16,4,256,256]{3,2,1,0:T(8,128)(2,1)} %gather_fusion.1, pred[16]{0:T(512)(128)(4,1)S(1)} %and_bitcast_fusion.4, pred[16]{0:T(512)(128)(4,1)S(1)} %and_bitcast_fusion.6, pred[4,16]{0,1:T(8,128)(4,1)S(1)} %broadcast_and_fusion.2, ...), kind=kLoop, calls=%fused_computation.13 | loop fusion | flops 29360128 | bytes 33554592 | tf_op jit(solution)/shard_map/add | solution.py:115
  176.2 16.4 %copy.147 = f32[1,4,256,16,256]{2,4,3,1,0:T(8,128)} copy(f32[1,4,256,16,256]{4,2,1,3,0:T(8,128)} %select_add_fusion.1) | data formatting | bytes 33554432 | tf_op jit(solution)/shard_map/add | solution.py:115
  204.5 31.8 %all-gather.11.cloned.1.call-done = f32[4,1,256,1024]{3,2,1,0:T(8,128)} async-done(((f32[1,1,256,1024]{3,2,1,0:T(8,128)}), f32[4,1,256,1024]{3,2,1,0:T(8,128)}) %all-gather.11.cloned.1.call-update) | async-done | bytes 4194320 | tf_op jit(solution)/shard_map/all_gather | solution.py:75
  248.3 11.7 custom-call.91
  260.6 9.8 custom-call.92
  276.9 12.1 custom-call.93
  290.2 9.8 custom-call.94
  303.4 11.7 custom-call.95
  316.4 9.8 custom-call.96
  329.8 11.9 custom-call.97
  343.0 9.8 custom-call.98
  356.3 11.7 custom-call.99
  369.3 10.0 custom-call.100
  382.7 11.7 custom-call.101
  395.7 9.8 custom-call.102
  408.5 12.1 custom-call.103
  421.8 9.8 custom-call.104
  434.2 11.7 custom-call.105
  459.8 28.1 %while.4 = (s32[]{:T(128)}, f32[1,1024,1024]{2,1,0:T(8,128)}, s32[8,2]{0,1:T(2,128)S(1)}, f32[8,1,128,128]{3,2,1,0:T(8,128)}, s32[]{:T(128)}) while((s32[]{:T(128)}, f32[1,1024,1024]{2,1,0:T(8,128)}, s32[8,2]{0,1:T(2,128)S(1)}, f32[8,1,128,128]{3,2,1,0:T(8,128)}, s32[]{:T(128)}) %tuple.131), condition=%wide.while_cond, body=%wide.while_body.sunk | while | flops 2 | bytes 132205 | solution.py:79
  487.9 80.2 %custom-call.106 = f32[1,8,128,128]{2,3,1,0:T(8,128)} custom-call(f32[1,8,128,128]{3,2,1,0:T(8,128)} %bitcast.938), custom_call_target="InvertDiagBlocksLowerTriangular" | custom-call | tf_op jit(solution)/shard_map/triangular_solve/custom-call.7 | solution.py:79
  612.0 10.1 copy.157
  622.0 28.0 %all-gather.7.cloned.1.call-done = bf16[4,1,3,256,1024]{4,3,2,1,0:T(8,128)(2,1)} async-done(((bf16[1,1,3,256,1024]{4,3,2,1,0:T(8,128)(2,1)}), bf16[4,1,3,256,1024]{4,3,2,1,0:T(8,128)(2,1)}) %all-gather.7.cloned.1.call-update) | async-done | bytes 6291472 | tf_op jit(solution)/shard_map/all_gather | solution.py:83
  667.5 11.2 collective-permute-done.3
  715.6 52.5 %collective-permute-done.2 = bf16[1,768,3072]{2,1,0:T(8,128)(2,1)} collective-permute-done((bf16[1,768,3072]{2,1,0:T(8,128)(2,1)}, bf16[1,768,3072]{2,1,0:T(8,128)(2,1)}, u32[]{:S(2)}, u32[]{:S(2)}) %collective-permute-start.2) | collective-permute-done | bytes 4718624 | tf_op jit(solution)/shard_map/ppermute | solution.py:18
  803.8 13.8 %select_add_fusion = f32[1,4,256,16,256]{4,2,1,3,0:T(8,128)} fusion(bf16[16,4,256,256]{3,2,1,0:T(8,128)(2,1)} %gather_fusion.7, bf16[16,4,256,256]{3,2,1,0:T(8,128)(2,1)} %gather_fusion.5, pred[16]{0:T(512)(128)(4,1)S(1)} %and_bitcast_fusion, pred[16]{0:T(512)(128)(4,1)S(1)} %and_bitcast_fusion.2, pred[4,16]{0,1:T(8,128)(4,1)S(1)} %broadcast_and_fusion, ...), kind=kLoop, calls=%fused_computation.12 | loop fusion | flops 29360128 | bytes 33554592 | tf_op jit(solution)/shard_map/add | solution.py:129
  817.6 16.4 %copy.164 = f32[1,4,256,16,256]{2,4,3,1,0:T(8,128)} copy(f32[1,4,256,16,256]{4,2,1,3,0:T(8,128)} %select_add_fusion) | data formatting | bytes 33554432 | tf_op jit(solution)/shard_map/add | solution.py:129
  845.2 30.3 %all-gather.13.cloned.1.call-done = f32[4,1,256,1024]{3,2,1,0:T(8,128)} async-done(((f32[1,1,256,1024]{3,2,1,0:T(8,128)}), f32[4,1,256,1024]{3,2,1,0:T(8,128)}) %all-gather.13.cloned.1.call-update) | async-done | bytes 4194320 | tf_op jit(solution)/shard_map/all_gather | solution.py:75
  887.5 11.7 custom-call.111
  899.9 9.8 custom-call.112
  916.1 12.1 custom-call.113
  929.5 9.8 custom-call.114
  942.6 11.7 custom-call.115
  955.6 9.8 custom-call.116
  969.0 11.9 custom-call.117
  982.2 9.8 custom-call.118
  995.5 11.7 custom-call.119
  1008.5 10.0 custom-call.120
  1021.8 11.7 custom-call.121
  1034.8 9.8 custom-call.122
  1047.6 12.1 custom-call.123
  1061.0 9.8 custom-call.124
  1073.4 11.7 custom-call.125
  1099.0 28.1 %while.5 = (s32[]{:T(128)}, f32[1,1024,1024]{2,1,0:T(8,128)}, s32[8,2]{0,1:T(2,128)S(1)}, f32[8,1,128,128]{3,2,1,0:T(8,128)}, s32[]{:T(128)}) while((s32[]{:T(128)}, f32[1,1024,1024]{2,1,0:T(8,128)}, s32[8,2]{0,1:T(2,128)S(1)}, f32[8,1,128,128]{3,2,1,0:T(8,128)}, s32[]{:T(128)}) %tuple.145), condition=%wide.while_cond.clone, body=%wide.while_body.clone.sunk | while | flops 2 | bytes 132205 | solution.py:79
  1127.1 80.2 %custom-call.126 = f32[1,8,128,128]{2,3,1,0:T(8,128)} custom-call(f32[1,8,128,128]{3,2,1,0:T(8,128)} %bitcast.937), custom_call_target="InvertDiagBlocksLowerTriangular" | custom-call | tf_op jit(solution)/shard_map/triangular_solve/custom-call.7 | solution.py:79
  1252.1 9.4 slice.400
  1261.5 9.8 copy.173
  1277.3 14.4 %all-gather.9.cloned.1.call-done = bf16[4,1,3,256,1024]{4,3,2,1,0:T(8,128)(2,1)} async-done(((bf16[1,1,3,256,1024]{4,3,2,1,0:T(8,128)(2,1)}), bf16[4,1,3,256,1024]{4,3,2,1,0:T(8,128)(2,1)}) %all-gather.9.cloned.1.call-update) | async-done | bytes 6291472 | tf_op jit(solution)/shard_map/all_gather | solution.py:83
  (339 shorter events, 451.2 us)
Async XLA Ops:
  7.2 11.6 copy-start
  7.2 229.2 %all-gather.11.cloned.1.call-start = ((), (), s32[]{:S(2)}) async-start(), calls=%async_computation.2 | async-start | bytes 5242880 | tf_op jit(solution)/shard_map/all_gather | solution.py:75
  8.7 9.7 copy-start.18
  8.7 10.2 copy-start.19
  8.7 10.4 copy-start.17
  8.8 183.8 %collective-permute-start.1 = (bf16[1,4,256,512]{2,3,1,0:T(8,128)(2,1)S(1)}, bf16[1,4,256,512]{2,3,1,0:T(8,128)(2,1)S(1)}, u32[]{:S(2)}, u32[]{:S(2)}) collective-permute-start(bf16[1,4,256,512]{2,3,1,0:T(8,128)(2,1)S(1)} %bitcast.931), channel_id=1, source_target_pairs={{0,4},{4,0},{8,12},{12,8},{16,20},{20,16},{24,28},{28,24},{1,5},{5... | collective-permute-start | bytes 3145736 | tf_op jit(solution)/shard_map/ppermute | solution.py:18
  18.4 117.8 %collective-permute-start = (bf16[1,3,256,3072]{2,3,1,0:T(8,128)(2,1)}, bf16[1,3,256,3072]{2,3,1,0:T(8,128)(2,1)}, u32[]{:S(2)}, u32[]{:S(2)}) collective-permute-start(bf16[1,3,256,3072]{2,3,1,0:T(8,128)(2,1)} %bitcast.890), channel_id=1, source_target_pairs={{0,4},{4,0},{8,12},{12,8},{16,20},{20,16},{24,28},{28,24},{1,5},{5... | collective-permute-start | bytes 14155784 | tf_op jit(solution)/shard_map/ppermute | solution.py:18
  196.9 2.0 copy-start.2
  200.2 1.9 slice-start
  200.2 449.8 %all-gather.7.cloned.1.call-start = ((), (), s32[]{:S(2)}) async-start(), calls=%async_computation | async-start | bytes 7864320 | tf_op jit(solution)/shard_map/all_gather | solution.py:83
  246.3 1.9 copy-start.10
  452.2 115.9 %copy-start.9 = (f32[1,3,256,1024]{3,2,1,0:T(8,128)S(1)}, f32[1,3,256,1024]{3,2,1,0:T(8,128)}, u32[]{:S(2)}) copy-start(f32[1,3,256,1024]{3,2,1,0:T(8,128)} %copy.153) | copy-start | bytes 9437188
  568.1 6.9 copy-start.14
  600.1 1.7 copy-start.4
  603.5 272.0 %all-gather.13.cloned.1.call-start = ((), (), s32[]{:S(2)}) async-start(), calls=%async_computation.3 | async-start | bytes 5242880 | tf_op jit(solution)/shard_map/all_gather | solution.py:75
  650.1 5.5 copy-start.12
  655.5 9.1 copy-start.16
  663.2 104.9 %collective-permute-start.2 = (bf16[1,768,3072]{2,1,0:T(8,128)(2,1)}, bf16[1,768,3072]{2,1,0:T(8,128)(2,1)}, u32[]{:S(2)}, u32[]{:S(2)}) collective-permute-start(bf16[1,768,3072]{2,1,0:T(8,128)(2,1)} %bitcast.930), channel_id=1, source_target_pairs={{0,8},{4,12},{8,0},{12,4},{16,24},{20,28},{24,16},{28,20},{1,9},{5... | collective-permute-start | bytes 14155784 | tf_op jit(solution)/shard_map/ppermute | solution.py:18
  664.8 13.9 %collective-permute-start.3 = (bf16[1,4,256,256]{2,3,1,0:T(8,128)(2,1)S(1)}, bf16[1,4,256,256]{2,3,1,0:T(8,128)(2,1)S(1)}, u32[]{:S(2)}, u32[]{:S(2)}) collective-permute-start(bf16[1,4,256,256]{2,3,1,0:T(8,128)(2,1)S(1)} %bitcast.927), channel_id=1, source_target_pairs={{0,4},{4,0},{8,12},{12,8},{16,20},{20,16},{24,28},{28,24},{1,5},{5... | collective-permute-start | bytes 1572872 | tf_op jit(solution)/shard_map/ppermute | solution.py:18
  679.0 155.0 %collective-permute-start.4 = (bf16[1,4,256,512]{2,3,1,0:T(8,128)(2,1)S(1)}, bf16[1,4,256,512]{2,3,1,0:T(8,128)(2,1)}, u32[]{:S(2)}, u32[]{:S(2)}) collective-permute-start(bf16[1,4,256,512]{2,3,1,0:T(8,128)(2,1)S(1)} %maximum_select_fusion.3), channel_id=1, source_target_pairs={{0,8},{4,12},{8,0},{12,4},{16,24},{20,28},{24,16},{28,20},{1,9},{5... | collective-permute-start | bytes 3145736 | tf_op jit(solution)/shard_map/ppermute | solution.py:18
  837.5 2.0 copy-start.3
  840.9 1.9 slice-start.1
  840.9 450.7 %all-gather.9.cloned.1.call-start = ((), (), s32[]{:S(2)}) async-start(), calls=%async_computation.1 | async-start | bytes 7864320 | tf_op jit(solution)/shard_map/all_gather | solution.py:83
  885.5 1.9 copy-start.11
  1091.4 115.9 %copy-start.8 = (f32[1,3,256,1024]{3,2,1,0:T(8,128)S(1)}, f32[1,3,256,1024]{3,2,1,0:T(8,128)}, u32[]{:S(2)}) copy-start(f32[1,3,256,1024]{3,2,1,0:T(8,128)} %copy.171) | copy-start | bytes 9437188
  1207.3 6.9 copy-start.15
  1239.3 1.7 copy-start.6
  1241.0 4.1 copy-start.5
  1261.5 9.8 copy-start.7
  1277.3 17.9 %copy-start.13 = (bf16[1,768,1024]{1,2,0:T(8,128)(2,1)S(1)}, bf16[1,768,1024]{1,2,0:T(8,128)(2,1)}, u32[]{:S(2)}) copy-start(bf16[1,768,1024]{1,2,0:T(8,128)(2,1)} %convert_element_type.105) | copy-start | bytes 4718596
  1295.2 8.1 copy-start.1
Sparse Core Ops, SparseCore 0:
  200.4 35.9 all-gather.10
  603.6 46.3 all-gather.6
  841.0 34.4 all-gather.12
  1245.2 46.3 all-gather.8
where the time goes:
time: 1320 us; the launch traced here: 1310 us
  other arithmetic  601 us (46%)
  local copies, waits for them, and re-layouts  297 us (22%)
  waiting for transfers between devices  257 us (19%)
  matrix products  123 us (9%)
  between operations  25.2 us (2%)
    another operation x62, other arithmetic, factor_front(): lower_factor = jnp.linalg.cholesky(pivot_block)  346 us
    another operation x5, other arithmetic, factor_front(): lax.linalg.triangular_solve(lower_factor, coupling, left_side=False, lowe...  174 us
    ppermute x5, waiting for transfers between devices, swapped(): return lax.ppermute(value, axis, pairs)  153 us
    another operation x30, matrix products, factor_front(): lax.linalg.triangular_solve(lower_factor, coupling, left_side=False, lowe...  63.7 us
    another operation x53, local copies, waits for them, and re-layouts, factor_front(): lax.linalg.triangular_solve(lower_factor, coupling, left_side=False, lowe...  62.8 us
    all_gather x2, waiting for transfers between devices, factor_front(): pivot_all = lax.all_gather(pivot_piece[None], 'front', axis=0, tiled=True)  62.1 us
    another operation x28, matrix products, factor_front(): lower_factor = jnp.linalg.cholesky(pivot_block)  46.3 us
    all_gather x2, waiting for transfers between devices, factor_front(): lax.all_gather(panel_round.reshape(batch_count, local_tiles, TILE, S)[Non...  42.4 us
  transfers between devices with their start and end apart: 9, of which 7 were waited for; matrix products, arithmetic and copies ran while one was open for 19% of the time, Pallas kernels for 0%

commit v1 on v0

--- a/solution.py
+++ b/solution.py
@@ -1,6 +1,8 @@
 import jax
 import jax.numpy as jnp
 from jax import lax
+from jax.experimental import pallas as pl
+from jax.experimental.pallas import tpu as pltpu
 from jax.sharding import PartitionSpec as P
 
 TILE = 256
@@ -10,6 +12,200 @@
 S = 1024
 U = 3072
 F = 4096
+BLK = 128
+GRP = 8
+NT = (((1,), (1,)), ((), ()))
+
+
+def halves(x):
+    high = x.astype(jnp.bfloat16)
+    low = (x - high.astype(jnp.float32)).astype(jnp.bfloat16)
+    return high, low
+
+
+def left_parts(x):
+    high, low = halves(x)
+    return jnp.concatenate([high, low, high], axis=1)
+
+
+def right_rows(x):
+    high, low = halves(x)
+    return jnp.concatenate([high, high, low], axis=0)
+
+
+def right_lanes(x):
+    high, low = halves(x)
+    return jnp.concatenate([high, high, low], axis=1)
+
+
+def dot_rows(left, right):
+    return jnp.dot(left, right, preferred_element_type=jnp.float32)
+
+
+def dot_lanes(left, right):
+    return lax.dot_general(left, right, NT, preferred_element_type=jnp.float32)
+
+
+def spread_row(ref, index):
+    return jnp.broadcast_to(ref[index], (GRP, BLK))
+
+
+def factor_diagonal(block, done_ref, pivot_ref, rows_ref):
+    steps = BLK // GRP
+    row_id = lax.broadcasted_iota(jnp.int32, (GRP, BLK), 0)
+    lane_id = lax.broadcasted_iota(jnp.int32, (GRP, BLK), 1)
+    matrix = [block[GRP * g : GRP * (g + 1), :] for g in range(steps)]
+    inverse = [jnp.where(lane_id == row_id + GRP * g, 1.0, 0.0).astype(jnp.float32) for g in range(steps)]
+    for g in range(steps):
+        first = GRP * g
+        slot = g % 2
+        current = matrix[g]
+        rows_ref[slot, :, 0:BLK] = current
+        rows_ref[slot, :, BLK:] = inverse[g]
+        for i in range(GRP):
+            pivot_ref[slot, i] = jnp.broadcast_to(current[:, first + i : first + i + 1], (GRP, BLK))
+        entry = {}
+        for m in range(GRP):
+            for i in range(m + 1):
+                entry[m, i] = jnp.broadcast_to(pivot_ref[slot, i, m : m + 1, :], (GRP, BLK))
+                entry[i, m] = entry[m, i]
+        left = [jnp.broadcast_to(rows_ref[slot, m : m + 1, 0:BLK], (GRP, BLK)) for m in range(GRP)]
+        right = [jnp.broadcast_to(rows_ref[slot, m : m + 1, BLK:], (GRP, BLK)) for m in range(GRP)]
+        for i in range(GRP):
+            root = lax.rsqrt(entry[i, i])
+            scale = root * root
+            done_ref[first + i : first + i + 1, 0:BLK] = (left[i] * root)[0:1]
+            done_ref[first + i : first + i + 1, BLK:] = (right[i] * root)[0:1]
+            left[i] = left[i] * scale
+            right[i] = right[i] * scale
+            scaled = {c: entry[i, c] * scale for c in range(i + 1, GRP)}
+            for m in range(GRP):
+                if m == i:
+                    continue
+                weight = entry[m, i]
+                left[m] = left[m] - weight * left[i]
+                right[m] = right[m] - weight * right[i]
+                for c in range(i + 1, GRP):
+                    if m > c:
+                        continue
+                    entry[m, c] = entry[m, c] - weight * scaled[c]
+            for m in range(i + 1, GRP):
+                for c in range(i + 1, m):
+                    entry[m, c] = entry[c, m]
+            for c in range(i + 1, GRP):
+                entry[i, c] = scaled[c]
+        for later in range(g + 1, steps):
+            rows = matrix[later]
+            total_left, total_right = None, None
+            for i in range(GRP):
+                weight = jnp.broadcast_to(rows[:, first + i : first + i + 1], (GRP, BLK))
+                part_left, part_right = weight * left[i], weight * right[i]
+                total_left = part_left if total_left is None else total_left + part_left
+                total_right = part_right if total_right is None else total_right + part_right
+            matrix[later] = rows - total_left
+            inverse[later] = inverse[later] - total_right
+
+
+def cholesky_kernel(pivot_ref, lower_ref, inverse_ref, work, done, block_inverse, entries, rows):
+    order = pivot_ref.shape[0]
+    blocks = order // BLK
+    work[...] = pivot_ref[...]
+    lower_ref[...] = jnp.zeros_like(lower_ref)
+    row_id = lax.broadcasted_iota(jnp.int32, (BLK, BLK), 0)
+    lane_id = lax.broadcasted_iota(jnp.int32, (BLK, BLK), 1)
+
+    def step(k, carry):
+        start = pl.multiple_of(k * BLK, BLK)
+        span = pl.ds(start, BLK)
+        factor_diagonal(work[span, span], done, entries, rows)
+        upper = jnp.where(lane_id >= row_id, done[:, 0:BLK], 0.0)
+        lower_ref[span, span] = upper.T
+        block_inverse[k] = done[:, BLK:]
+        for fixed in range(blocks - 1):
+            after = (fixed + 1) * BLK
+
+            @pl.when(k == fixed)
+            def _():
+                strip = dot_rows(
+                    left_parts(done[:, BLK:]), right_rows(work[after - BLK : after, after:])
+                )
+                column = strip.T
+                lower_ref[after:, after - BLK : after] = column
+                left = left_parts(column)
+                right = right_rows(strip)
+                width = order - after
+                for top in range(0, width, TILE):
+                    high = min(TILE, width - top)
+                    work[after + top : after + top + high, after + top :] = work[
+                        after + top : after + top + high, after + top :
+                    ] - dot_rows(left[top : top + high], right[:, top:])
+
+        return carry
+
+    lax.fori_loop(0, blocks, step, 0)
+    for tile in range(order // TILE):
+        base = tile * TILE
+        first, second = block_inverse[2 * tile], block_inverse[2 * tile + 1]
+        corner = lower_ref[base + BLK : base + TILE, base : base + BLK]
+        mixed = dot_rows(left_parts(corner), right_rows(first))
+        mixed = -dot_rows(left_parts(second), right_rows(mixed))
+        inverse_ref[tile, 0:BLK, 0:BLK] = first
+        inverse_ref[tile, 0:BLK, BLK:] = jnp.zeros((BLK, BLK), jnp.float32)
+        inverse_ref[tile, BLK:, 0:BLK] = mixed
+        inverse_ref[tile, BLK:, BLK:] = second
+
+
+def cholesky(pivot):
+    order = pivot.shape[0]
+    return pl.pallas_call(
+        cholesky_kernel,
+        out_shape=(
+            jax.ShapeDtypeStruct((order, order), jnp.float32),
+            jax.ShapeDtypeStruct((order // TILE, TILE, TILE), jnp.float32),
+        ),
+        in_specs=[pl.BlockSpec(memory_space=pltpu.VMEM)],
+        out_specs=(pl.BlockSpec(memory_space=pltpu.VMEM), pl.BlockSpec(memory_space=pltpu.VMEM)),
+        scratch_shapes=[
+            pltpu.VMEM((order, order), jnp.float32),
+            pltpu.VMEM((BLK, 2 * BLK), jnp.float32),
+            pltpu.VMEM((order // BLK, BLK, BLK), jnp.float32),
+            pltpu.VMEM((2, GRP, GRP, BLK), jnp.float32),
+            pltpu.VMEM((2, GRP, 2 * BLK), jnp.float32),
+        ],
+        compiler_params=pltpu.CompilerParams(vmem_limit_bytes=40 * 2**20),
+        name="cholesky",
+    )(pivot)
+
+
+def panel_kernel(coupling_ref, lower_ref, inverse_ref, panel_ref):
+    order = lower_ref.shape[0]
+    solved = []
+    for k in range(order // TILE):
+        span = slice(k * TILE, (k + 1) * TILE)
+        rest = coupling_ref[:, span]
+        if k:
+            left = jnp.concatenate([part[0] for part in solved], axis=1)
+            low = jnp.concatenate([part[1] for part in solved], axis=1)
+            high_lower, low_lower = halves(lower_ref[span, 0 : k * TILE])
+            rest = rest - dot_lanes(
+                jnp.concatenate([left, low, left], axis=1),
+                jnp.concatenate([high_lower, high_lower, low_lower], axis=1),
+            )
+        block = dot_lanes(left_parts(rest), right_lanes(inverse_ref[k]))
+        panel_ref[:, span] = block
+        solved.append(halves(block))
+
+
+def solve_panel(coupling, lower, inverse):
+    spec = pl.BlockSpec(memory_space=pltpu.VMEM)
+    return pl.pallas_call(
+        panel_kernel,
+        out_shape=jax.ShapeDtypeStruct(coupling.shape, jnp.float32),
+        in_specs=[spec, spec, spec],
+        out_specs=spec,
+        compiler_params=pltpu.CompilerParams(vmem_limit_bytes=40 * 2**20),
+        name="panel",
+    )(coupling, lower, inverse)
 
 
 def swapped(value, axis, apart):
@@ -74,10 +270,12 @@
     pivot_piece = canvas[:, :1, :, :S]
     pivot_all = lax.all_gather(pivot_piece[None], "front", axis=0, tiled=True)
     pivot_block = jnp.moveaxis(pivot_all, 0, 2).reshape(batch_count, S, S)
-    lower_factor = jnp.linalg.cholesky(pivot_block)
+    lower_factor, inverse = (
+        jnp.stack(parts) for parts in zip(*[cholesky(pivot_block[b]) for b in range(batch_count)])
+    )
     coupling = canvas[:, 1:, :, :S].reshape(batch_count, local_tiles * TILE, S)
-    panel_full = lax.linalg.triangular_solve(
-        lower_factor, coupling, left_side=False, lower=True, transpose_a=True
+    panel_full = jnp.stack(
+        [solve_panel(coupling[b], lower_factor[b], inverse[b]) for b in range(batch_count)]
     )
     panel_round = panel_full.astype(jnp.bfloat16)
     shared = lax.all_gather(

time: 1320 us -> 681 us (0.52)
  other arithmetic: 601 us -> 76.8 us
  matrix products: 123 us -> 18.2 us
  Pallas kernels: 0 us -> 87.7 us
  local copies, waits for them, and re-layouts: 297 us -> 211 us
    another operation x67 -> x0, other arithmetic: 520 us -> none  [the longest x62 346 us: factor_front(): lower_factor = jnp.linalg.cholesky(pivot_block)]
    another operation x58 -> x0, matrix products: 110 us -> none  [the longest x30 63.7 us: factor_front(): lax.linalg.triangular_solve(lower_factor, coupling, left_side=False, lowe...]
    pallas_call x0 -> x4, Pallas kernels: none -> 87.7 us  [the longest x2 76.1 us: cholesky(): pl.pallas_call(cholesky_kernel, out_shape=(jax.ShapeDtypeStruct((order, o...]
    another operation x71 -> x0, local copies, waits for them, and re-layouts: 78.9 us -> none  [the longest x53 62.8 us: factor_front(): lax.linalg.triangular_solve(lower_factor, coupling, left_side=False, lowe...]
  transfers between devices with their start and end apart: 9 -> 9, of which waited for: 7 -> 7; matrix products, arithmetic and copies ran while one was open for 19% -> 38% of each run, Pallas kernels for 0% -> 0%
where the time goes in v1:
time: 681 us; the launch traced here: 672 us
  waiting for transfers between devices  257 us (38%)
  local copies, waits for them, and re-layouts  211 us (31%)
  Pallas kernels  87.7 us (13%)
  other arithmetic  76.8 us (11%)
  matrix products  18.2 us (3%)
  between operations  14.7 us (2%)
  starting transfers between devices  7.13 us (1%)
    ppermute x5, waiting for transfers between devices, swapped(): return lax.ppermute(value, axis, pairs)  145 us
    pallas_call x2, Pallas kernels, cholesky(): pl.pallas_call(cholesky_kernel, out_shape=(jax.ShapeDtypeStruct((order, o...  76.1 us
    all_gather x2, waiting for transfers between devices, factor_front(): pivot_all = lax.all_gather(pivot_piece[None], 'front', axis=0, tiled=True)  60.4 us
    all_gather x2, waiting for transfers between devices, factor_front(): lax.all_gather(panel_round.reshape(batch_count, local_tiles, TILE, S)[Non...  50.6 us
    another operation x5, local copies, waits for them, and re-layouts, place_child(): blocks = child_rows.reshape(batch_count, local_tiles, TILE, UT, TILE)  38.6 us
    slice x4, local copies, waits for them, and re-layouts, factor_front(): trailing = canvas[:, 1:, :, S:].reshape(batch_count, local_tiles * TILE, U)  37.1 us
    gather x8, local copies, waits for them, and re-layouts, place_tiles(): taken = jnp.take(taken, col_source, axis=2)  30.4 us
    select_n x4, other arithmetic, place_tiles(): taken = jnp.take(blocks, row_source, axis=0)  24.5 us
  transfers between devices with their start and end apart: 9, of which 7 were waited for; matrix products, arithmetic and copies ran while one was open for 38% of the time, Pallas kernels for 0%

profile of v1, /device:TPU:0, one launch (start us, length us, event | category | flops | bytes accessed | tf_op | source)
XLA Modules:
  0.0 672.1 jit_solution(6565700549820369323)
XLA Ops:
  8.8 3.0 collective-permute-start.1
  11.8 6.6 copy.102
  19.8 6.6 copy.103
  26.8 6.0 gather_fusion
  33.0 6.2 bitcast_select_fusion.7
  39.2 7.5 %gather_fusion.1 = bf16[16,4,256,256]{3,2,1,0:T(8,128)(2,1)} fusion(bf16[1,4,256,12,256]{4,2,3,1,0:T(8,128)(2,1)} %bitcast_select_fusion.7, s32[16]{0:T(128)S(1)} %or_bitcast_fusion.6), kind=kCustom, calls=%fused_computation.1.clone | custom fusion | bytes 16777344 | tf_op jit(solution)/shard_map/vmap(jit(_take))/gather | solution.py:219
  47.4 88.8 %collective-permute-done = bf16[1,3,256,3072]{2,3,1,0:T(8,128)(2,1)} collective-permute-done((bf16[1,3,256,3072]{2,3,1,0:T(8,128)(2,1)}, bf16[1,3,256,3072]{2,3,1,0:T(8,128)(2,1)}, u32[]{:S(2)}, u32[]{:S(2)}) %collective-permute-start) | collective-permute-done | bytes 4718624 | tf_op jit(solution)/shard_map/ppermute | solution.py:214
  136.1 6.6 copy.108
  142.8 5.9 gather_fusion.2
  148.7 6.1 bitcast_select_fusion.6
  154.8 7.5 %gather_fusion.3 = bf16[16,4,256,256]{3,2,1,0:T(8,128)(2,1)} fusion(bf16[1,4,256,12,256]{4,2,3,1,0:T(8,128)(2,1)} %bitcast_select_fusion.6, s32[16]{0:T(128)S(1)} %or_bitcast_fusion.4), kind=kCustom, calls=%fused_computation.5.clone | custom fusion | bytes 16777344 | tf_op jit(solution)/shard_map/vmap(jit(_take))/gather | solution.py:219
  162.4 13.8 %select_add_fusion.1 = f32[1,4,256,16,256]{4,2,1,3,0:T(8,128)} fusion(bf16[16,4,256,256]{3,2,1,0:T(8,128)(2,1)} %gather_fusion.3, bf16[16,4,256,256]{3,2,1,0:T(8,128)(2,1)} %gather_fusion.1, pred[16]{0:T(512)(128)(4,1)S(1)} %and_bitcast_fusion.4, pred[16]{0:T(512)(128)(4,1)S(1)} %and_bitcast_fusion.6, pred[4,16]{0,1:T(8,128)(4,1)S(1)} %broadcast_and_fusion.2, ...), kind=kLoop, calls=%fused_computation.9 | loop fusion | flops 29360128 | bytes 33554592 | tf_op jit(solution)/shard_map/add | solution.py:313
  176.2 16.4 %copy.109 = f32[1,4,256,16,256]{2,4,3,1,0:T(8,128)} copy(f32[1,4,256,16,256]{4,2,1,3,0:T(8,128)} %select_add_fusion.1) | data formatting | bytes 33554432 | tf_op jit(solution)/shard_map/add | solution.py:313
  192.5 4.3 slice_add_fusion.1
  205.5 33.2 %all-gather.11.cloned.1.call-done = f32[4,1,256,1024]{3,2,1,0:T(8,128)} async-done(((f32[1,1,256,1024]{3,2,1,0:T(8,128)}), f32[4,1,256,1024]{3,2,1,0:T(8,128)}) %all-gather.11.cloned.1.call-update) | async-done | bytes 4194320 | tf_op jit(solution)/shard_map/all_gather | solution.py:271
  241.0 37.9 %cholesky.2 = (f32[1024,1024]{1,0:T(8,128)S(1)}, f32[4,256,256]{2,1,0:T(8,128)S(1)}) custom-call(f32[1024,1024]{1,0:T(8,128)S(1)} %bitcast.238), custom_call_target="tpu_custom_call" | custom-call | tf_op jit(solution)/shard_map/cholesky/pallas_call | solution.py:160
  279.0 5.8 panel.2
  286.2 8.4 %slice.71 = f32[1,3,256,3072]{2,3,1,0:T(8,128)} slice(f32[1,4,256,4096]{2,3,1,0:T(8,128)} %bitcast.243), slice={[0:1], [1:4], [0:256], [1024:4096]} | slice | bytes 18874368 | tf_op jit(solution)/shard_map/slice | solution.py:291
  294.7 9.8 %copy.116 = f32[1,3,256,3072]{3,2,1,0:T(8,128)} copy(f32[1,3,256,3072]{2,3,1,0:T(8,128)} %slice.71) | data formatting | bytes 18874368 | tf_op jit(solution)/shard_map/slice | solution.py:291
  304.5 28.3 %all-gather.7.cloned.1.call-done = bf16[4,1,3,256,1024]{4,3,0,2,1:T(8,128)(2,1)} async-done(((bf16[1,1,3,256,1024]{4,3,0,2,1:T(8,128)(2,1)}), bf16[4,1,3,256,1024]{4,3,0,2,1:T(8,128)(2,1)}) %all-gather.7.cloned.1.call-update) | async-done | bytes 6291472 | tf_op jit(solution)/shard_map/all_gather | solution.py:281
  332.7 10.5 %fusion = bf16[768,3072]{1,0:T(8,128)(2,1)} fusion(f32[1,3,256,3072]{3,2,1,0:T(8,128)} %copy.116, bf16[768,1024]{1,0:T(8,128)(2,1)} %convert_element_type.99, bf16[3072,1024]{1,0:T(8,128)(2,1)} %bitcast.262), kind=kOutput, calls=%fused_computation.11 | convolution fusion | flops 4836556800 | bytes 22020096 | tf_op jit(solution)/shard_map/brk,bnk->brn/dot_general | solution.py:292
  349.3 11.6 %collective-permute-done.3 = bf16[1,4,256,256]{2,3,1,0:T(8,128)(2,1)} collective-permute-done((bf16[1,4,256,256]{2,3,1,0:T(8,128)(2,1)}, bf16[1,4,256,256]{2,3,1,0:T(8,128)(2,1)}, u32[]{:S(2)}, u32[]{:S(2)}) %collective-permute-start.3) | collective-permute-done | bytes 524320 | tf_op jit(solution)/shard_map/ppermute | solution.py:214
  360.9 3.0 maximum_select_fusion.3
  364.4 3.0 fusion.6
  367.4 9.2 %reshape_reshape.6 = bf16[1,3,256,12,256]{4,3,2,1,0:T(8,128)(2,1)} reshape(bf16[768,3072]{1,0:T(8,128)(2,1)} %fusion) | data formatting | bytes 9437184 | tf_op jit(solution)/shard_map/reshape;reshape | solution.py:243
  376.5 6.8 %copy.118 = bf16[1,3,256,12,256]{4,2,3,1,0:T(8,128)(2,1)} copy(bf16[1,3,256,12,256]{4,3,2,1,0:T(8,128)(2,1)} %reshape_reshape.6) | data formatting | bytes 9437184 | tf_op jit(solution)/shard_map/reshape;reshape | solution.py:243
  383.3 6.0 gather_fusion.4
  389.3 6.2 bitcast_select_fusion.5
  395.5 7.6 %gather_fusion.5 = bf16[16,4,256,256]{3,2,1,0:T(8,128)(2,1)} fusion(bf16[1,4,256,12,256]{4,2,3,1,0:T(8,128)(2,1)} %bitcast_select_fusion.5, s32[16]{0:T(128)S(1)} %or_bitcast_fusion.2), kind=kCustom, calls=%fused_computation.6.clone | custom fusion | bytes 16777344 | tf_op jit(solution)/shard_map/vmap(jit(_take))/gather | solution.py:219
  403.1 45.1 %collective-permute-done.2 = bf16[1,768,3072]{2,1,0:T(8,128)(2,1)} collective-permute-done((bf16[1,768,3072]{2,1,0:T(8,128)(2,1)}, bf16[1,768,3072]{2,1,0:T(8,128)(2,1)}, u32[]{:S(2)}, u32[]{:S(2)}) %collective-permute-start.2) | collective-permute-done | bytes 4718624 | tf_op jit(solution)/shard_map/ppermute | solution.py:214
  448.2 9.2 %reshape_reshape.7 = bf16[1,3,256,12,256]{4,3,2,1,0:T(8,128)(2,1)} reshape(bf16[1,768,3072]{2,1,0:T(8,128)(2,1)} %collective-permute-done.2) | data formatting | bytes 9437184 | tf_op jit(solution)/shard_map/reshape;reshape | solution.py:243
  457.4 6.8 %copy.121 = bf16[1,3,256,12,256]{4,2,3,1,0:T(8,128)(2,1)} copy(bf16[1,3,256,12,256]{4,3,2,1,0:T(8,128)(2,1)} %reshape_reshape.7) | data formatting | bytes 9437184 | tf_op jit(solution)/shard_map/reshape;reshape | solution.py:243
  464.2 5.9 gather_fusion.6
  470.1 6.1 bitcast_select_fusion.4
  476.2 7.7 %gather_fusion.7 = bf16[16,4,256,256]{3,2,1,0:T(8,128)(2,1)} fusion(bf16[1,4,256,12,256]{4,2,3,1,0:T(8,128)(2,1)} %bitcast_select_fusion.4, s32[16]{0:T(128)S(1)} %or_bitcast_fusion), kind=kCustom, calls=%fused_computation.7.clone | custom fusion | bytes 16777344 | tf_op jit(solution)/shard_map/vmap(jit(_take))/gather | solution.py:219
  483.9 13.8 %select_add_fusion = f32[1,4,256,16,256]{4,2,1,3,0:T(8,128)} fusion(bf16[16,4,256,256]{3,2,1,0:T(8,128)(2,1)} %gather_fusion.7, bf16[16,4,256,256]{3,2,1,0:T(8,128)(2,1)} %gather_fusion.5, pred[16]{0:T(512)(128)(4,1)S(1)} %and_bitcast_fusion, pred[16]{0:T(512)(128)(4,1)S(1)} %and_bitcast_fusion.2, pred[4,16]{0,1:T(8,128)(4,1)S(1)} %broadcast_and_fusion, ...), kind=kLoop, calls=%fused_computation.8 | loop fusion | flops 29360128 | bytes 33554592 | tf_op jit(solution)/shard_map/add | solution.py:327
  497.7 16.4 %copy.122 = f32[1,4,256,16,256]{2,4,3,1,0:T(8,128)} copy(f32[1,4,256,16,256]{4,2,1,3,0:T(8,128)} %select_add_fusion) | data formatting | bytes 33554432 | tf_op jit(solution)/shard_map/add | solution.py:327
  514.1 4.2 slice_add_fusion
  523.9 3.8 slice.74
  527.8 3.6 copy.127
  531.4 27.2 %all-gather.13.cloned.1.call-done = f32[4,1,256,1024]{3,2,1,0:T(8,128)} async-done(((f32[1,1,256,1024]{3,2,1,0:T(8,128)}), f32[4,1,256,1024]{3,2,1,0:T(8,128)}) %all-gather.13.cloned.1.call-update) | async-done | bytes 4194320 | tf_op jit(solution)/shard_map/all_gather | solution.py:271
  560.9 38.2 %cholesky.3 = (f32[1024,1024]{1,0:T(8,128)S(1)}, f32[4,256,256]{2,1,0:T(8,128)S(1)}) custom-call(f32[1024,1024]{1,0:T(8,128)S(1)} %bitcast.239), custom_call_target="tpu_custom_call" | custom-call | tf_op jit(solution)/shard_map/cholesky/pallas_call | solution.py:160
  599.1 5.8 panel.3
  610.9 9.1 %slice.75 = f32[1,3,256,3072]{2,3,1,0:T(8,128)} slice(f32[1,4,256,4096]{2,3,1,0:T(8,128)} %bitcast.241), slice={[0:1], [1:4], [0:256], [1024:4096]} | slice | bytes 18874368 | tf_op jit(solution)/shard_map/slice | solution.py:291
  619.9 9.8 %copy.128 = f32[1,3,256,3072]{3,2,1,0:T(8,128)} copy(f32[1,3,256,3072]{2,3,1,0:T(8,128)} %slice.75) | data formatting | bytes 18874368 | tf_op jit(solution)/shard_map/slice | solution.py:291
  632.1 22.4 %all-gather.9.cloned.1.call-done = bf16[4,1,3,256,1024]{4,3,0,2,1:T(8,128)(2,1)} async-done(((bf16[1,1,3,256,1024]{4,3,0,2,1:T(8,128)(2,1)}), bf16[4,1,3,256,1024]{4,3,0,2,1:T(8,128)(2,1)}) %all-gather.9.cloned.1.call-update) | async-done | bytes 6291472 | tf_op jit(solution)/shard_map/all_gather | solution.py:281
  654.5 7.7 %fusion.37 = f32[768,3072]{1,0:T(8,128)S(1)} fusion(bf16[768,1024]{1,0:T(8,128)(2,1)} %convert_element_type.107, bf16[3072,1024]{1,0:T(8,128)(2,1)} %bitcast.261), kind=kOutput, calls=%fused_computation.137 | convolution fusion | flops 4831838208 | bytes 17301504 | tf_op jit(solution)/shard_map/brk,bnk->brn/dot_general | solution.py:292
  662.2 3.0 fusion.1
  (128 shorter events, 39.2 us)
Async XLA Ops:
  7.2 11.6 %copy-start = (s32[4,1,12,4]{2,3,1,0:T(4,128)S(1)}, s32[4,1,12,4]{2,3,1,0:T(4,128)}, u32[]{:S(2)}) copy-start(s32[4,1,12,4]{2,3,1,0:T(4,128)} %param.16) | copy-start | bytes 2308
  7.2 231.5 %all-gather.11.cloned.1.call-start = ((), (), s32[]{:S(2)}) async-start(), calls=%async_computation.2 | async-start | bytes 5242880 | tf_op jit(solution)/shard_map/all_gather | solution.py:271
  8.7 9.7 %copy-start.13 = (s32[4,1,4,3]{2,1,3,0:T(1,128)S(1)}, s32[4,1,4,3]{2,1,3,0:T(1,128)}, u32[]{:S(2)}) copy-start(s32[4,1,4,3]{2,1,3,0:T(1,128)} %param.15) | copy-start | bytes 580
  8.7 10.2 %copy-start.14 = (s32[2,1,12,4]{2,3,1,0:T(4,128)S(1)}, s32[2,1,12,4]{2,3,1,0:T(4,128)}, u32[]{:S(2)}) copy-start(s32[2,1,12,4]{2,3,1,0:T(4,128)} %param.17) | copy-start | bytes 1156
  8.7 10.4 %copy-start.12 = (s32[8,1,4,3]{0,2,3,1:T(4,128)S(1)}, s32[8,1,4,3]{0,2,3,1:T(4,128)}, u32[]{:S(2)}) copy-start(s32[8,1,4,3]{0,2,3,1:T(4,128)} %param.14) | copy-start | bytes 1156
  8.8 183.8 %collective-permute-start.1 = (bf16[1,4,256,512]{2,3,1,0:T(8,128)(2,1)S(1)}, bf16[1,4,256,512]{2,3,1,0:T(8,128)(2,1)S(1)}, u32[]{:S(2)}, u32[]{:S(2)}) collective-permute-start(bf16[1,4,256,512]{2,3,1,0:T(8,128)(2,1)S(1)} %bitcast.252), channel_id=1, source_target_pairs={{0,4},{4,0},{8,12},{12,8},{16,20},{20,16},{24,28},{28,24},{1,5},{5... | collective-permute-start | bytes 3145736 | tf_op jit(solution)/shard_map/ppermute | solution.py:214
  18.4 117.8 %collective-permute-start = (bf16[1,3,256,3072]{2,3,1,0:T(8,128)(2,1)}, bf16[1,3,256,3072]{2,3,1,0:T(8,128)(2,1)}, u32[]{:S(2)}, u32[]{:S(2)}) collective-permute-start(bf16[1,3,256,3072]{2,3,1,0:T(8,128)(2,1)} %bitcast.244), channel_id=1, source_target_pairs={{0,4},{4,0},{8,12},{12,8},{16,20},{20,16},{24,28},{28,24},{1,5},{5... | collective-permute-start | bytes 14155784 | tf_op jit(solution)/shard_map/ppermute | solution.py:214
  196.9 2.0 copy-start.10
  199.9 3.2 slice-start
  202.6 130.2 %all-gather.7.cloned.1.call-start = ((), (), s32[]{:S(2)}) async-start(), calls=%async_computation | async-start | bytes 7864320 | tf_op jit(solution)/shard_map/all_gather | solution.py:281
  238.7 40.3 %copy-start.4 = (f32[1,3,256,1024]{3,2,1,0:T(8,128)S(1)}, f32[1,3,256,1024]{3,2,1,0:T(8,128)}, u32[]{:S(2)}) copy-start(f32[1,3,256,1024]{3,2,1,0:T(8,128)} %copy.113) | copy-start | bytes 9437188
  238.7 2.3 copy-start.8
  279.0 5.8 copy-start.6
  286.2 272.3 %all-gather.13.cloned.1.call-start = ((), (), s32[]{:S(2)}) async-start(), calls=%async_computation.3 | async-start | bytes 5242880 | tf_op jit(solution)/shard_map/all_gather | solution.py:271
  343.2 104.9 %collective-permute-start.2 = (bf16[1,768,3072]{2,1,0:T(8,128)(2,1)}, bf16[1,768,3072]{2,1,0:T(8,128)(2,1)}, u32[]{:S(2)}, u32[]{:S(2)}) collective-permute-start(bf16[1,768,3072]{2,1,0:T(8,128)(2,1)} %bitcast.68), channel_id=1, source_target_pairs={{0,8},{4,12},{8,0},{12,4},{16,24},{20,28},{24,16},{28,20},{1,9},{5... | collective-permute-start | bytes 14155784 | tf_op jit(solution)/shard_map/ppermute | solution.py:214
  346.8 14.1 %collective-permute-start.3 = (bf16[1,4,256,256]{2,3,1,0:T(8,128)(2,1)}, bf16[1,4,256,256]{2,3,1,0:T(8,128)(2,1)}, u32[]{:S(2)}, u32[]{:S(2)}) collective-permute-start(bf16[1,4,256,256]{2,3,1,0:T(8,128)(2,1)} %bitcast.249), channel_id=1, source_target_pairs={{0,4},{4,0},{8,12},{12,8},{16,20},{20,16},{24,28},{28,24},{1,5},{5... | collective-permute-start | bytes 1572872 | tf_op jit(solution)/shard_map/ppermute | solution.py:214
  363.9 150.2 %collective-permute-start.4 = (bf16[1,4,256,512]{2,3,1,0:T(8,128)(2,1)}, bf16[1,4,256,512]{2,3,1,0:T(8,128)(2,1)}, u32[]{:S(2)}, u32[]{:S(2)}) collective-permute-start(bf16[1,4,256,512]{2,3,1,0:T(8,128)(2,1)} %maximum_select_fusion.3), channel_id=1, source_target_pairs={{0,8},{4,12},{8,0},{12,4},{16,24},{20,28},{24,16},{28,20},{1,9},{5... | collective-permute-start | bytes 3145736 | tf_op jit(solution)/shard_map/ppermute | solution.py:214
  518.3 2.0 copy-start.11
  523.9 130.6 %all-gather.9.cloned.1.call-start = ((), (), s32[]{:S(2)}) async-start(), calls=%async_computation.1 | async-start | bytes 7864320 | tf_op jit(solution)/shard_map/all_gather | solution.py:281
  558.5 40.6 %copy-start.5 = (f32[1,3,256,1024]{3,2,1,0:T(8,128)S(1)}, f32[1,3,256,1024]{3,2,1,0:T(8,128)}, u32[]{:S(2)}) copy-start(f32[1,3,256,1024]{3,2,1,0:T(8,128)} %copy.127) | copy-start | bytes 9437188
  558.5 2.3 copy-start.9
  599.1 5.8 copy-start.7
  604.9 1.7 copy-start.2
  619.9 11.1 %copy-start.3 = (f32[768,1024]{1,0:T(8,128)S(1)}, f32[768,1024]{1,0:T(8,128)}, u32[]{:S(2)}) copy-start(f32[768,1024]{1,0:T(8,128)} %copy-done.2) | copy-start | bytes 9437188
  654.5 10.7 %copy-start.1 = (s32[4,1,12,4]{2,3,1,0:T(4,128)S(1)}, s32[4,1,12,4]{2,3,1,0:T(4,128)}, u32[]{:S(2)}) copy-start(s32[4,1,12,4]{2,3,1,0:T(4,128)} %param.16) | copy-start | bytes 2308
Sparse Core Ops, SparseCore 0:
  202.7 35.9 all-gather.10
  286.3 46.3 all-gather.6
  524.0 34.4 all-gather.12
  608.1 46.3 all-gather.8

commit v2 on v1

v2 whole, which is shorter than its diff:
```python
import jax
import jax.numpy as jnp
from jax import lax
from jax.experimental import pallas as pl
from jax.experimental.pallas import tpu as pltpu
from jax.sharding import PartitionSpec as P

S = 1024
BLK = 128
GRP = 8
TILE = 256
NT = (((1,), (1,)), ((), ()))


def halves(x):
    high = x.astype(jnp.bfloat16)
    low = (x - high.astype(jnp.float32)).astype(jnp.bfloat16)
    return high, low


def left_parts(x):
    high, low = halves(x)
    return jnp.concatenate([high, low, high], axis=1)


def right_rows(x):
    high, low = halves(x)
    return jnp.concatenate([high, high, low], axis=0)


def right_lanes(x):
    high, low = halves(x)
    return jnp.concatenate([high, high, low], axis=1)


def dot_rows(left, right):
    return jnp.dot(left, right, preferred_element_type=jnp.float32)


def dot_lanes(left, right):
    return lax.dot_general(left, right, NT, preferred_element_type=jnp.float32)


def spread_row(ref, index):
    return jnp.broadcast_to(ref[index], (GRP, BLK))


def factor_diagonal(block, done_ref, pivot_ref, rows_ref):
    steps = BLK // GRP
    row_id = lax.broadcasted_iota(jnp.int32, (GRP, BLK), 0)
    lane_id = lax.broadcasted_iota(jnp.int32, (GRP, BLK), 1)
    matrix = [block[GRP * g : GRP * (g + 1), :] for g in range(steps)]
    inverse = [jnp.where(lane_id == row_id + GRP * g, 1.0, 0.0).astype(jnp.float32) for g in range(steps)]
    for g in range(steps):
        first = GRP * g
        slot = g % 2
        current = matrix[g]
        rows_ref[slot, :, 0:BLK] = current
        rows_ref[slot, :, BLK:] = inverse[g]
        for i in range(GRP):
            pivot_ref[slot, i] = jnp.broadcast_to(current[:, first + i : first + i + 1], (GRP, BLK))
        entry = {}
        for m in range(GRP):
            for i in range(m + 1):
                entry[m, i] = jnp.broadcast_to(pivot_ref[slot, i, m : m + 1, :], (GRP, BLK))
                entry[i, m] = entry[m, i]
        left = [jnp.broadcast_to(rows_ref[slot, m : m + 1, 0:BLK], (GRP, BLK)) for m in range(GRP)]
        right = [jnp.broadcast_to(rows_ref[slot, m : m + 1, BLK:], (GRP, BLK)) for m in range(GRP)]
        for i in range(GRP):
            root = lax.rsqrt(entry[i, i])
            scale = root * root
            done_ref[first + i : first + i + 1, 0:BLK] = (left[i] * root)[0:1]
            done_ref[first + i : first + i + 1, BLK:] = (right[i] * root)[0:1]
            left[i] = left[i] * scale
            right[i] = right[i] * scale
            scaled = {c: entry[i, c] * scale for c in range(i + 1, GRP)}
            for m in range(GRP):
                if m == i:
                    continue
                weight = entry[m, i]
                left[m] = left[m] - weight * left[i]
                right[m] = right[m] - weight * right[i]
                for c in range(i + 1, GRP):
                    if m > c:
                        continue
                    entry[m, c] = entry[m, c] - weight * scaled[c]
            for m in range(i + 1, GRP):
                for c in range(i + 1, m):
                    entry[m, c] = entry[c, m]
            for c in range(i + 1, GRP):
                entry[i, c] = scaled[c]
        for later in range(g + 1, steps):
            rows = matrix[later]
            total_left, total_right = None, None
            for i in range(GRP):
                weight = jnp.broadcast_to(rows[:, first + i : first + i + 1], (GRP, BLK))
                part_left, part_right = weight * left[i], weight * right[i]
                total_left = part_left if total_left is None else total_left + part_left
                total_right = part_right if total_right is None else total_right + part_right
            matrix[later] = rows - total_left
            inverse[later] = inverse[later] - total_right


def cholesky_kernel(pivot_ref, lower_ref, inverse_ref, work, done, block_inverse, entries, rows):
    order = pivot_ref.shape[0]
    blocks = order // BLK
    work[...] = pivot_ref[...]
    lower_ref[...] = jnp.zeros_like(lower_ref)
    row_id = lax.broadcasted_iota(jnp.int32, (BLK, BLK), 0)
    lane_id = lax.broadcasted_iota(jnp.int32, (BLK, BLK), 1)

    def step(k, carry):
        start = pl.multiple_of(k * BLK, BLK)
        span = pl.ds(start, BLK)
        factor_diagonal(work[span, span], done, entries, rows)
        upper = jnp.where(lane_id >= row_id, done[:, 0:BLK], 0.0)
        lower_ref[span, span] = upper.T
        block_inverse[k] = done[:, BLK:]
        for fixed in range(blocks - 1):
            after = (fixed + 1) * BLK

            @pl.when(k == fixed)
            def _():
                strip = dot_rows(
                    left_parts(done[:, BLK:]), right_rows(work[after - BLK : after, after:])
                )
                column = strip.T
                lower_ref[after:, after - BLK : after] = column
                left = left_parts(column)
                right = right_rows(strip)
                width = order - after
                for top in range(0, width, TILE):
                    high = min(TILE, width - top)
                    work[after + top : after + top + high, after + top :] = work[
                        after + top : after + top + high, after + top :
                    ] - dot_rows(left[top : top + high], right[:, top:])

        return carry

    lax.fori_loop(0, blocks, step, 0)
    for tile in range(order // TILE):
        base = tile * TILE
        first, second = block_inverse[2 * tile], block_inverse[2 * tile + 1]
        corner = lower_ref[base + BLK : base + TILE, base : base + BLK]
        mixed = dot_rows(left_parts(corner), right_rows(first))
        mixed = -dot_rows(left_parts(second), right_rows(mixed))
        inverse_ref[tile, 0:BLK, 0:BLK] = first
        inverse_ref[tile, 0:BLK, BLK:] = jnp.zeros((BLK, BLK), jnp.float32)
        inverse_ref[tile, BLK:, 0:BLK] = mixed
        inverse_ref[tile, BLK:, BLK:] = second


def cholesky(pivot):
    order = pivot.shape[0]
    return pl.pallas_call(
        cholesky_kernel,
        out_shape=(
            jax.ShapeDtypeStruct((order, order), jnp.float32),
            jax.ShapeDtypeStruct((order // TILE, TILE, TILE), jnp.float32),
        ),
        in_specs=[pl.BlockSpec(memory_space=pltpu.VMEM)],
        out_specs=(pl.BlockSpec(memory_space=pltpu.VMEM), pl.BlockSpec(memory_space=pltpu.VMEM)),
        scratch_shapes=[
            pltpu.VMEM((order, order), jnp.float32),
            pltpu.VMEM((BLK, 2 * BLK), jnp.float32),
            pltpu.VMEM((order // BLK, BLK, BLK), jnp.float32),
            pltpu.VMEM((2, GRP, GRP, BLK), jnp.float32),
            pltpu.VMEM((2, GRP, 2 * BLK), jnp.float32),
        ],
        compiler_params=pltpu.CompilerParams(vmem_limit_bytes=40 * 2**20),
        name="cholesky",
    )(pivot)


VMEM = pl.BlockSpec(memory_space=pltpu.VMEM)
SMEM = pl.BlockSpec(memory_space=pltpu.SMEM)
ANY = pl.BlockSpec(memory_space=pl.ANY)
GROUPS = 4
PARAMS = pltpu.CompilerParams(vmem_limit_bytes=48 * 2**20)


def swapped(value, axis, apart):
    mask = 2**apart
    pairs = [(source, source ^ mask) for source in range(lax.axis_size(axis))]
    return lax.ppermute(value, axis, pairs)


def find_tile(map_ref, owner, group, slot, count):
    base = (owner * GROUPS + group) * count
    found = jnp.int32(-1)
    for s in range(count):
        found = jnp.where(map_ref[base + s] == slot, jnp.int32(s), found)
    return found


def column_targets(half, side):
    targets = []
    for part in (side, 1 - side):
        targets.append(2 * part + 1 - half)
        targets += [4 + 3 * (2 * part + half) + i for i in range(3)]
    return targets


def share_place(target, half):
    place = jnp.int32(0)
    for other in column_targets(half, 0):
        earlier = jnp.logical_and((other & 3) == (target & 3), other < target)
        place = place + earlier.astype(jnp.int32)
    return place


def start_tile(live, source, zero, target, sem):
    @pl.when(live)
    def _():
        pltpu.make_async_copy(source, target, sem).start()

    @pl.when(jnp.logical_not(live))
    def _():
        pltpu.make_async_copy(zero, target, sem).start()


def pick_separator_kernel(ids_ref, map_ref, child_ref, entries_ref, pivot_ref, coupling_ref, zero, sems, entry_sems):
    count = child_ref.shape[0]
    leaf, column = ids_ref[0], ids_ref[1]
    width = GROUPS * TILE
    first_entries = pltpu.make_async_copy(entries_ref.at[0], pivot_ref.at[:, pl.ds(width, width // 2)], entry_sems.at[0])
    other_entries = pltpu.make_async_copy(
        entries_ref.at[pl.ds(1, count)], coupling_ref.at[:, :, pl.ds(width, width // 2)], entry_sems.at[1]
    )
    first_entries.start()
    zero[...] = jnp.zeros_like(zero)
    waits = []
    for slot in range(count + 1):
        row = find_tile(map_ref, leaf, column, slot, count)
        for group in range(GROUPS):
            place = find_tile(map_ref, leaf, group, 0, count)
            live = jnp.logical_and(row >= 0, place >= 0)
            source = child_ref.at[
                jnp.maximum(row, 0),
                :,
                pl.ds(pl.multiple_of((jnp.maximum(place, 0) * GROUPS + group) * TILE, TILE), TILE),
            ]
            span = pl.ds(group * TILE, TILE)
            target = pivot_ref.at[:, span] if slot == 0 else coupling_ref.at[slot - 1, :, span]
            sem = sems.at[slot * GROUPS + group]
            start_tile(live, source, zero, target, sem)
            waits.append(pltpu.make_async_copy(zero, target, sem))
    other_entries.start()
    for wait in waits:
        wait.wait()
    first_entries.wait()
    other_entries.wait()


def pick_separator(ids, child_map, child, entries):
    count, _, _ = child.shape
    width = GROUPS * TILE + entries.shape[-1]
    return pl.pallas_call(
        pick_separator_kernel,
        out_shape=(
            jax.ShapeDtypeStruct((TILE, width), child.dtype),
            jax.ShapeDtypeStruct((count, TILE, width), child.dtype),
        ),
        in_specs=[SMEM, SMEM, ANY, ANY],
        out_specs=(ANY, ANY),
        scratch_shapes=[
            pltpu.VMEM((TILE, TILE), child.dtype),
            pltpu.SemaphoreType.DMA(((count + 1) * GROUPS,)),
            pltpu.SemaphoreType.DMA((2,)),
        ],
        compiler_params=pltpu.CompilerParams(vmem_limit_bytes=4 * 2**20),
        name="pick_separator",
    )(ids, child_map, child, entries)


def pick_trailing_kernel(ids_ref, map_ref, next_ref, child_ref, send_ref, keep_ref, zero, sems):
    count = child_ref.shape[0]
    leaf, column = ids_ref[0], ids_ref[1]
    pair = leaf >> 1
    zero[...] = jnp.zeros_like(zero)
    rows = [find_tile(map_ref, leaf, column, slot, count) for slot in range(1, count + 1)]
    waits = []
    for which, (device, out_ref) in enumerate(((leaf ^ 1, send_ref), (leaf, keep_ref))):
        for position, target in enumerate(column_targets(device & 1, (device >> 1) & 1)):
            group = target & 3
            update = find_tile(next_ref, pair, group, target >> 2, count)
            place = find_tile(map_ref, leaf, group, update + 1, count)
            column_live = jnp.logical_and(update >= 0, place >= 0)
            source_span = pl.ds(pl.multiple_of((jnp.maximum(place, 0) * GROUPS + group) * TILE, TILE), TILE)
            for slot, row in enumerate(rows):
                live = jnp.logical_and(column_live, row >= 0)
                source = child_ref.at[jnp.maximum(row, 0), :, source_span]
                goal = out_ref.at[slot, :, pl.ds(position * TILE, TILE)]
                sem = sems.at[(which * 8 + position) * count + slot]
                start_tile(live, source, zero, goal, sem)
                waits.append(pltpu.make_async_copy(zero, goal, sem))
    for wait in waits:
        wait.wait()


def pick_trailing(ids, child_map, next_map, child):
    count = child.shape[0]
    shape = jax.ShapeDtypeStruct((count, TILE, 8 * TILE), child.dtype)
    return pl.pallas_call(
        pick_trailing_kernel,
        out_shape=(shape, shape),
        in_specs=[SMEM, SMEM, SMEM, ANY],
        out_specs=(ANY, ANY),
        scratch_shapes=[pltpu.VMEM((TILE, TILE), child.dtype), pltpu.SemaphoreType.DMA((16 * count,))],
        compiler_params=pltpu.CompilerParams(vmem_limit_bytes=4 * 2**20),
        name="pick_trailing",
    )(ids, child_map, next_map, child)


def solve_blocks(coupling_ref, lower_ref, inverse_ref, panel_ref):
    order = lower_ref.shape[0]
    solved = []
    for k in range(order // TILE):
        span = slice(k * TILE, (k + 1) * TILE)
        rest = coupling_ref[:, span]
        if k:
            left = jnp.concatenate([part[0] for part in solved], axis=1)
            low = jnp.concatenate([part[1] for part in solved], axis=1)
            high_lower, low_lower = halves(lower_ref[span, 0 : k * TILE])
            rest = rest - dot_lanes(
                jnp.concatenate([left, low, left], axis=1),
                jnp.concatenate([high_lower, high_lower, low_lower], axis=1),
            )
        block = dot_lanes(left_parts(rest), right_lanes(inverse_ref[k]))
        panel_ref[:, span] = block
        solved.append(halves(block))
    return jnp.concatenate([part[0] for part in solved], axis=1)


def write_factor(column, offset, lower_ref, panel, factor_ref):
    width = factor_ref.shape[-1]
    rows = pl.ds(pl.multiple_of(column * TILE, TILE), TILE)
    span = pl.ds(pl.multiple_of(offset * width, width), width)
    factor_ref[0] = lower_ref[rows, span]
    for s in range(factor_ref.shape[0] - 1):
        factor_ref[s + 1] = panel[s * TILE : (s + 1) * TILE, span]


def panel_one_kernel(
    ids_ref, mask_ref, next_ref, mine_ref, peer_ref, lower_ref, inverse_ref, factor_ref, round_ref, share_ref, coupling, panel
):
    leaf, column = ids_ref[0], ids_ref[1]
    half, pair = leaf & 1, leaf >> 1
    count = mine_ref.shape[0]
    order = lower_ref.shape[0]
    for s in range(count):
        for tile in range(order // TILE):
            span = slice(tile * TILE, (tile + 1) * TILE)
            where = order + (tile % 2) * TILE
            weight = mask_ref[((pair * count + s) * GROUPS + column) * GROUPS + tile].astype(jnp.float32)
            mine = mine_ref[s, :, where : where + TILE].astype(jnp.float32)
            peer = peer_ref[s, :, where : where + TILE].astype(jnp.float32)
            own_first = half == tile // 2
            entry = jnp.where(own_first, mine, peer)
            coupling[s * TILE : (s + 1) * TILE, span] = (
                mine_ref[s, :, span].astype(jnp.float32) + peer_ref[s, :, span].astype(jnp.float32) + entry * weight
            )
    rounded = solve_blocks(coupling, lower_ref, inverse_ref, panel)
    for s in range(count):
        round_ref[s] = rounded[s * TILE : (s + 1) * TILE]
    write_factor(column, half, lower_ref, panel, factor_ref)
    for a in range(2):
        slot = jnp.int32(0)
        for target in column_targets(half, 0):
            hit = jnp.logical_and((target & 3) == column, share_place(target, half) == a)
            slot = jnp.where(hit, target >> 2, slot)
        tile = find_tile(next_ref, pair, column, slot, count)
        share_ref[a] = round_ref[jnp.maximum(tile, 0)]


def panel_one(ids, mask, next_map, mine, peer, lower, inverse):
    count = mine.shape[0]
    order = lower.shape[0]
    return pl.pallas_call(
        panel_one_kernel,
        out_shape=(
            jax.ShapeDtypeStruct((count + 1, TILE, order // 2), jnp.float32),
            jax.ShapeDtypeStruct((count, TILE, order), jnp.bfloat16),
            jax.ShapeDtypeStruct((2, TILE, order), jnp.bfloat16),
        ),
        in_specs=[SMEM, SMEM, SMEM, VMEM, VMEM, VMEM, VMEM],
        out_specs=(VMEM, VMEM, VMEM),
        scratch_shapes=[
            pltpu.VMEM((count * TILE, order), jnp.float32),
            pltpu.VMEM((count * TILE, order), jnp.float32),
        ],
        compiler_params=PARAMS,
        name="panel_one",
    )(ids, mask, next_map, mine, peer, lower, inverse)


def panel_two_kernel(ids_ref, own_ref, x_ref, z_ref, both_ref, lower_ref, inverse_ref, factor_ref, round_ref, share_ref, coupling, panel):
    leaf, column = ids_ref[0], ids_ref[1]
    half, side = leaf & 1, (leaf >> 1) & 1
    quarter = leaf & 3
    count = round_ref.shape[0]
    for place, ref in (
        (2 * side + 1 - half, own_ref),
        (2 * side + half, x_ref),
        (2 * (1 - side) + 1 - half, z_ref),
        (2 * (1 - side) + half, both_ref),
    ):
        coupling[:, pl.ds(pl.multiple_of(place * TILE, TILE), TILE)] = ref[...]
    rounded = solve_blocks(coupling, lower_ref, inverse_ref, panel)
    for s in range(count):
        round_ref[s] = rounded[s * TILE : (s + 1) * TILE]
    write_factor(column, quarter, lower_ref, panel, factor_ref)
    chosen = jnp.int32(0)
    for i in range(3):
        tile = 3 * quarter + i
        chosen = jnp.where((tile & 3) == column, tile >> 2, chosen)
    share_ref[...] = round_ref[chosen]


def panel_two(ids, parts, lower, inverse):
    rows = parts[0].shape[0]
    count = rows // TILE
    order = lower.shape[0]
    return pl.pallas_call(
        panel_two_kernel,
        out_shape=(
            jax.ShapeDtypeStruct((count + 1, TILE, order // 4), jnp.float32),
            jax.ShapeDtypeStruct((count, TILE, order), jnp.bfloat16),
            jax.ShapeDtypeStruct((TILE, order), jnp.bfloat16),
        ),
        in_specs=[SMEM] + [VMEM] * 6,
        out_specs=(VMEM, VMEM, VMEM),
        scratch_shapes=[pltpu.VMEM((rows, order), jnp.float32), pltpu.VMEM((rows, order), jnp.float32)],
        compiler_params=PARAMS,
        name="panel_two",
    )(ids, *parts, lower, inverse)


def update_one_kernel(
    ids_ref, next_ref, keep_ref, peer_ref, round_ref, shared_ref,
    far_pivot_ref, far_coupling_ref, far_trailing_ref, near_pivot_ref, near_coupling_ref, near_trailing_ref, tiles
):
    leaf, column = ids_ref[0], ids_ref[1]
    half, side, pair = leaf & 1, (leaf >> 1) & 1, leaf >> 1
    count = keep_ref.shape[0]
    step = pl.program_id(0)
    group = 1 - step // 4
    inner = step % 4
    targets = column_targets(half, side)
    target = targets[0]
    for position in range(1, 8):
        target = jnp.where(group * 4 + inner == position, targets[position], target)
    live = find_tile(next_ref, pair, target & 3, target >> 2, count) >= 0
    shared = shared_ref[(target & 3) * 2 + share_place(target, half)]
    for s in range(count):
        value = keep_ref[s].astype(jnp.float32) + peer_ref[s].astype(jnp.float32) - dot_lanes(round_ref[s], shared)
        tiles[s] = jnp.where(live, value, 0.0).astype(jnp.bfloat16)
    tiles[count] = jnp.zeros_like(tiles[count])

    def placed(slot):
        row = find_tile(next_ref, pair, column, slot, count)
        return tiles[jnp.where(row < 0, count, row)]

    for which, pivot_ref, coupling_ref, trailing_ref in (
        (1, far_pivot_ref, far_coupling_ref, far_trailing_ref),
        (0, near_pivot_ref, near_coupling_ref, near_trailing_ref),
    ):

        @pl.when(jnp.logical_and(group == which, inner == 0))
        def _():
            pivot_ref[...] = placed(0)
            for slot in range(1, count + 1):
                coupling_ref[slot - 1] = placed(slot)

        @pl.when(jnp.logical_and(group == which, inner > 0))
        def _():
            for slot in range(1, count + 1):
                trailing_ref[slot - 1] = placed(slot)


def update_one(ids, next_map, keep, peer, rounded, shared):
    count, _, order = rounded.shape
    column_of = lambda step: (0, 0, (1 - step // 4) * 4 + step % 4)
    far_of = lambda step: (0, 0, jnp.clip(step - 1, 0, 2))
    near_of = lambda step: (0, 0, jnp.clip(step - 5, 0, 2))
    fixed2 = lambda step: (0, 0)
    fixed3 = lambda step: (0, 0, 0)
    tile_spec = pl.BlockSpec((TILE, TILE), fixed2)
    coupling_spec = pl.BlockSpec((count, TILE, TILE), fixed3)
    shapes = (
        jax.ShapeDtypeStruct((TILE, TILE), jnp.bfloat16),
        jax.ShapeDtypeStruct((count, TILE, TILE), jnp.bfloat16),
        jax.ShapeDtypeStruct((count, TILE, 3 * TILE), jnp.bfloat16),
    )
    return pl.pallas_call(
        update_one_kernel,
        grid=(8,),
        out_shape=shapes + shapes,
        in_specs=[
            SMEM,
            SMEM,
            pl.BlockSpec((count, TILE, TILE), column_of),
            pl.BlockSpec((count, TILE, TILE), column_of),
            VMEM,
            VMEM,
        ],
        out_specs=(
            tile_spec, coupling_spec, pl.BlockSpec((count, TILE, TILE), far_of),
            tile_spec, coupling_spec, pl.BlockSpec((count, TILE, TILE), near_of),
        ),
        scratch_shapes=[pltpu.VMEM((count + 1, TILE, TILE), jnp.bfloat16)],
        compiler_params=PARAMS,
        name="update_one",
    )(ids, next_map, keep, peer, rounded, shared)


def update_two_kernel(ids_ref, near_ref, far_ref, round_ref, shared_ref, out_ref):
    quarter = ids_ref[0] & 3
    for i in range(3):
        shared = shared_ref[(3 * quarter + i) & 3]
        span = slice(i * TILE, (i + 1) * TILE)
        for s in range(near_ref.shape[0]):
            total = near_ref[s, :, span].astype(jnp.float32) + far_ref[s, :, span].astype(jnp.float32)
            out_ref[s, :, span] = (total - dot_lanes(round_ref[s], shared)).astype(jnp.bfloat16)


def update_two(ids, near, far, rounded, shared):
    return pl.pallas_call(
        update_two_kernel,
        out_shape=jax.ShapeDtypeStruct(near.shape, jnp.bfloat16),
        in_specs=[SMEM, VMEM, VMEM, VMEM, VMEM],
        out_specs=VMEM,
        compiler_params=PARAMS,
        name="update_two",
    )(ids, near, far, rounded, shared)


def in_order(mine, other, mine_first):
    return jnp.where(
        mine_first, jnp.concatenate([mine, other], axis=-1), jnp.concatenate([other, mine], axis=-1)
    )


def body(child_update, sep_one, sep_two, map_one, map_two, mask_one, mask_two):
    column = lax.axis_index("front")
    leaf = lax.axis_index("leaf")
    half, side, pair, quad = leaf & 1, (leaf >> 1) & 1, leaf >> 1, leaf >> 2
    ids = jnp.stack([leaf, column]).astype(jnp.int32)
    child = child_update[0, 0, 0]
    entries_one = sep_one[0, 0, 0]
    entries_two = sep_two[0, 0, 0]
    count = child.shape[0]
    maps_one = map_one.reshape(-1)
    maps_two = map_two.reshape(-1)

    pivot_mine, coupling_mine = pick_separator(ids, maps_one, child, entries_one)
    pivot_peer = swapped(pivot_mine, "leaf", 0)
    coupling_peer = swapped(coupling_mine, "leaf", 0)
    send, keep = pick_trailing(ids, maps_one, maps_two, child)
    trailing_peer = swapped(send, "leaf", 0)
    entries_near = swapped(entries_two, "leaf", 0)

    wide = pivot_mine.astype(jnp.float32)
    wide_peer = pivot_peer.astype(jnp.float32)
    pivot_rows = wide[:, :S] + wide_peer[:, :S] + in_order(wide[:, S:], wide_peer[:, S:], half == 0)
    pivot = lax.all_gather(pivot_rows, "front", axis=0, tiled=True)
    lower, inverse = cholesky(pivot)
    factor_one, rounded, share = panel_one(
        ids, mask_one.reshape(-1), maps_two, coupling_mine, coupling_peer, lower, inverse
    )
    shared = lax.all_gather(share, "front", axis=0, tiled=True)
    far_pivot, far_coupling, far_trailing, near_pivot, near_coupling, near_trailing = update_one(
        ids, maps_two, keep, trailing_peer, rounded, shared
    )

    pivot_far = swapped(far_pivot, "leaf", 1)
    coupling_far = swapped(far_coupling, "leaf", 1)
    trailing_far = swapped(far_trailing, "leaf", 1)
    pivot_tile = (
        near_pivot.astype(jnp.float32) + pivot_far.astype(jnp.float32) + entries_near[0].astype(jnp.float32)
    )
    pivot_pair = in_order(pivot_tile, swapped(pivot_tile, "leaf", 0), half == 1)
    pivot_rows = in_order(pivot_pair, swapped(pivot_pair, "leaf", 1), side == 0)
    pivot = lax.all_gather(pivot_rows, "front", axis=0, tiled=True)
    mask_second = lax.dynamic_index_in_dim(mask_two, quad, 0, keepdims=False).reshape(count, GROUPS, -1)
    mask_second = lax.dynamic_index_in_dim(mask_second, column, 1, keepdims=False)
    mask_second = lax.dynamic_index_in_dim(mask_second, 2 * side + 1 - half, 1, keepdims=False)
    coupling = (
        near_coupling.astype(jnp.float32)
        + coupling_far.astype(jnp.float32)
        + entries_near[1:].astype(jnp.float32) * mask_second.astype(jnp.float32)[:, None, None]
    ).reshape(count * TILE, TILE)
    coupling_x = swapped(coupling, "leaf", 0)
    coupling_z, coupling_xz = swapped((coupling, coupling_x), "leaf", 1)
    lower, inverse = cholesky(pivot)
    factor_two, rounded, share = panel_two(
        ids, (coupling, coupling_x, coupling_z, coupling_xz), lower, inverse
    )
    shared = lax.all_gather(share[None], "front", axis=0, tiled=True)
    update = update_two(ids, near_trailing, trailing_far, rounded, shared)
    return (factor_one[None, None, None], factor_two[None, None, None], update[None, None, None])


def solution(mesh):
    split = P("leaf", "front", None, None, None, None)
    return jax.shard_map(
        body,
        mesh=mesh,
        in_specs=(split, split, split, P(), P(), P(), P()),
        out_specs=(split, split, split),
        check_vma=False,
    )
```

time: 681 us -> 370 us (0.54); the launches traced: 672 us -> 369 us
  local copies, waits for them, and re-layouts: 211 us -> 24.1 us
  other arithmetic: 76.8 us -> 7.68 us
  waiting for transfers between devices: 257 us -> 188 us
  Pallas kernels: 87.7 us -> 114 us
  matrix products: 18.2 us -> 0 us
  starting transfers between devices: 7.13 us -> 21.1 us
    all_gather x4, waiting for transfers between devices: 111 us -> 43.9 us  [the longest x2 43.9 us: body(): pivot = lax.all_gather(pivot_rows, 'front', axis=0, tiled=True)]
    gather x15 -> x0, local copies, waits for them, and re-layouts: 54.3 us -> none  [the longest x8 30.4 us: place_tiles(): taken = jnp.take(taken, col_source, axis=2)]
    slice x13 -> x2, local copies, waits for them, and re-layouts: 54.2 us -> 1.85 us  [the longest x1 1 us: body(): wide_peer[:, S:]]
    another operation x5 -> x0, local copies, waits for them, and re-layouts: 38.6 us -> none  [place_child(): blocks = child_rows.reshape(batch_count, local_tiles, TILE, UT, TILE)]
    add x2 -> x0, local copies, waits for them, and re-layouts: 32.7 us -> none  [the longest x1 16.4 us: body(): place_child(child_rows, map_own, column)]
    add x7 -> x3, other arithmetic: 36.2 us -> 3.6 us  [the longest x1 1.42 us: body(): wide[:, :S] + wide_peer[:, :S]]
    select_n x5 -> x2, other arithmetic: 27.5 us -> 1.19 us  [in_order(): jnp.where(mine_first, jnp.concatenate([mine, other], axis=-1), jnp.concat...]
    pallas_call x2 -> x6, Pallas kernels: 11.6 us -> 37.8 us  [the longest x1 10.8 us: panel_one(): pl.pallas_call(panel_one_kernel, out_shape=(jax.ShapeDtypeStruct((count +...]
  transfers between devices with their start and end apart: 9 -> 16, of which waited for: 7 -> 10; matrix products, arithmetic and copies ran while one was open for 38% -> 1% of each run, Pallas kernels for 0% -> 24%
where the time goes in v2:
time: 370 us; the launch traced here: 369 us
  waiting for transfers between devices  188 us (51%)
  Pallas kernels  114 us (31%)
  local copies, waits for them, and re-layouts  24.1 us (7%)
  starting transfers between devices  21.1 us (6%)
  between operations  14 us (4%)
  other arithmetic  7.68 us (2%)
    ppermute x12, waiting for transfers between devices, swapped(): return lax.ppermute(value, axis, pairs)  144 us
    pallas_call x2, Pallas kernels, cholesky(): pl.pallas_call(cholesky_kernel, out_shape=(jax.ShapeDtypeStruct((order, o...  76.3 us
    all_gather x2, waiting for transfers between devices, body(): pivot = lax.all_gather(pivot_rows, 'front', axis=0, tiled=True)  43.9 us
    unnamed x45, local copies, waits for them, and re-layouts  21.8 us
    ppermute x12, starting transfers between devices, swapped(): return lax.ppermute(value, axis, pairs)  20.9 us
    pallas_call x1, Pallas kernels, panel_one(): pl.pallas_call(panel_one_kernel, out_shape=(jax.ShapeDtypeStruct((count +...  10.8 us
    pallas_call x1, Pallas kernels, panel_two(): pl.pallas_call(panel_two_kernel, out_shape=(jax.ShapeDtypeStruct((count +...  10.1 us
    pallas_call x1, Pallas kernels, update_one(): pl.pallas_call(update_one_kernel, grid=(8,), out_shape=shapes + shapes, i...  9.99 us
  transfers between devices with their start and end apart: 16, of which 10 were waited for; matrix products, arithmetic and copies ran while one was open for 1% of the time, Pallas kernels for 24%

profile of v2, /device:TPU:0, one launch (start us, length us, event | category | flops | bytes accessed | tf_op | source)
XLA Modules:
  0.0 369.2 jit_solution(15611635506107186163)
XLA Ops:
  8.2 2.3 copy-done.1
  10.6 1.2 copy-done.12
  11.8 1.3 pick_separator.1
  13.1 3.0 collective-permute-start.1
  16.1 1.3 convert_element_type.31
  17.4 0.9 slice.26
  18.3 15.5 %collective-permute-done.1 = bf16[256,1536]{1,0:T(8,128)(2,1)} collective-permute-done((bf16[256,1536]{1,0:T(8,128)(2,1)S(1)}, bf16[256,1536]{1,0:T(8,128)(2,1)}, u32[]{:S(2)}, u32[]{:S(2)}) %collective-permute-start.1) | collective-permute-done | bytes 786464 | tf_op jit(solution)/shard_map/ppermute | solution.py:185
  33.8 1.3 convert_element_type.32
  35.1 1.0 slice.27
  36.1 1.4 fusion
  37.6 1.8 collective-permute-start
  39.9 33.8 %all-gather.6.cloned.1.call-done.pivot_ref = f32[1024,1024]{1,0:T(8,128)} async-done(((f32[256,1024]{1,0:T(8,128)}), f32[1024,1024]{1,0:T(8,128)}) %all-gather.6.cloned.1.call-update) | async-done | bytes 4194320 | tf_op jit(solution)/shard_map/all_gather | solution.py:566
  73.6 2.2 copy-done.4
  75.8 38.1 %cholesky.2 = (f32[1024,1024]{1,0:T(8,128)S(1)}, f32[4,256,256]{2,1,0:T(8,128)S(1)}) custom-call(f32[1024,1024]{1,0:T(8,128)S(1)} %copy-done.4), custom_call_target="tpu_custom_call" | custom-call | tf_op jit(solution)/shard_map/cholesky/pallas_call | solution.py:155
  114.0 1.9 copy-done.6
  115.9 10.8 %panel_one.1 = (f32[4,256,512]{2,1,0:T(8,128)}, bf16[3,256,1024]{2,1,0:T(8,128)(2,1)S(1)}, bf16[2,256,1024]{2,1,0:T(8,128)(2,1)}) custom-call(s32[2]{0:T(128)S(1)} %pad_add_fusion.ids_ref, s32[192]{0:T(256)S(1)} %reshape.26.mask_ref, s32[48]{0:T(128)S(1)} %reshape.27.next_ref, bf16[3,256,1536]{2,1,0:T(8,128)(2,1)S(1)} %get-tuple-element.23.mine_ref, ...), custom_call_target="tpu_custom_call" | custom-call | tf_op jit(solution)/shard_map/panel_one/pallas_call | solution.py:379
  126.7 1.2 copy-done.9
  128.0 2.3 copy-done.2
  130.3 2.6 pick_trailing.1
  132.9 1.6 copy-done.7
  134.5 1.5 collective-permute-start.2
  136.5 69.0 %collective-permute-done.2.peer_ref = bf16[3,256,2048]{2,1,0:T(8,128)(2,1)} collective-permute-done((bf16[3,256,2048]{2,1,0:T(8,128)(2,1)S(1)}, bf16[3,256,2048]{2,1,0:T(8,128)(2,1)}, u32[]{:S(2)}, u32[]{:S(2)}) %collective-permute-start.2) | collective-permute-done | bytes 3145760 | tf_op jit(solution)/shard_map/ppermute | solution.py:185
  205.6 10.0 %update_one.1 = (bf16[256,256]{1,0:T(8,128)(2,1)S(1)}, bf16[3,256,256]{2,1,0:T(8,128)(2,1)S(1)}, bf16[3,256,768]{2,1,0:T(8,128)(2,1)S(1)}, bf16[256,256]{1,0:T(8...) custom-call(s32[2]{0:T(128)S(1)} %pad_add_fusion.ids_ref, s32[48]{0:T(128)S(1)} %reshape.27.next_ref, ...), custom_call_target="tpu_custom_call" | custom-call | tf_op jit(solution)/shard_map/update_one/pallas_call | solution.py:495
  215.6 1.5 collective-permute-start.8
  217.1 3.5 collective-permute-done.8
  220.6 1.0 convert_add_fusion
  221.6 1.6 collective-permute-start.9
  223.2 4.8 %collective-permute-done.9 = f32[256,256]{1,0:T(8,128)S(1)} collective-permute-done((f32[256,256]{1,0:T(8,128)S(1)}, f32[256,256]{1,0:T(8,128)S(1)}, u32[]{:S(2)}, u32[]{:S(2)}) %collective-permute-start.9) | collective-permute-done | bytes 262176 | tf_op jit(solution)/shard_map/ppermute | solution.py:185
  228.1 1.5 collective-permute-start.10
  229.6 9.2 %collective-permute-done.10 = f32[256,512]{1,0:T(8,128)S(1)} collective-permute-done((f32[256,512]{1,0:T(8,128)S(1)}, f32[256,512]{1,0:T(8,128)S(1)}, u32[]{:S(2)}, u32[]{:S(2)}) %collective-permute-start.10) | collective-permute-done | bytes 524320 | tf_op jit(solution)/shard_map/ppermute | solution.py:185
  238.8 1.2 maximum_select_fusion.1
  240.0 1.7 collective-permute-start.3
  242.0 6.1 %collective-permute-done.3 = bf16[3,256,256]{2,1,0:T(8,128)(2,1)S(1)} collective-permute-done((bf16[3,256,256]{2,1,0:T(8,128)(2,1)S(1)}, bf16[3,256,256]{2,1,0:T(8,128)(2,1)S(1)}, u32[]{:S(2)}, u32[]{:S(2)}) %collective-permute-start.3) | collective-permute-done | bytes 393248 | tf_op jit(solution)/shard_map/ppermute | solution.py:185
  248.1 1.2 multiply_add_fusion
  249.3 2.9 collective-permute-start.5
  252.2 1.6 collective-permute-start.6
  253.8 9.4 %collective-permute-done.5.x_ref = f32[768,256]{1,0:T(8,128)S(1)} collective-permute-done((f32[768,256]{1,0:T(8,128)S(1)}, f32[768,256]{1,0:T(8,128)S(1)}, u32[]{:S(2)}, u32[]{:S(2)}) %collective-permute-start.5) | collective-permute-done | bytes 786464 | tf_op jit(solution)/shard_map/ppermute | solution.py:185
  263.2 1.7 collective-permute-start.7
  264.8 10.1 %all-gather.10.cloned.1.call-done.pivot_ref = f32[1024,1024]{1,0:T(8,128)} async-done(((f32[256,1024]{1,0:T(8,128)}), f32[1024,1024]{1,0:T(8,128)}) %all-gather.10.cloned.1.call-update) | async-done | bytes 4194320 | tf_op jit(solution)/shard_map/all_gather | solution.py:584
  275.0 2.2 copy-done.3
  277.2 38.2 %cholesky.3 = (f32[1024,1024]{1,0:T(8,128)S(1)}, f32[4,256,256]{2,1,0:T(8,128)S(1)}) custom-call(f32[1024,1024]{1,0:T(8,128)S(1)} %copy-done.3), custom_call_target="tpu_custom_call" | custom-call | tf_op jit(solution)/shard_map/cholesky/pallas_call | solution.py:155
  315.4 1.9 copy-done.5
  317.3 10.1 %panel_two.1 = (f32[4,256,256]{2,1,0:T(8,128)}, bf16[3,256,1024]{2,1,0:T(8,128)(2,1)}, bf16[256,1024]{1,0:T(8,128)(2,1)S(1)}) custom-call(s32[2]{0:T(128)S(1)} %pad_add_fusion.ids_ref, f32[768,256]{1,0:T(8,128)S(1)} %bitcast.27, f32[768,256]{1,0:T(8,128)S(1)} %collective-permute-done.5.x_ref, f32[768,256]{1,0:T(8,128)S(1)} %collective-permute-done.6.z_ref, ...), custom_call_target="tpu_custom_call" | custom-call | tf_op jit(solution)/shard_map/panel_two/pallas_call | solution.py:424
  328.2 1.6 collective-permute-start.11
  329.8 26.8 %collective-permute-done.11.far_ref = bf16[3,256,768]{2,1,0:T(8,128)(2,1)S(1)} collective-permute-done((bf16[3,256,768]{2,1,0:T(8,128)(2,1)}, bf16[3,256,768]{2,1,0:T(8,128)(2,1)S(1)}, u32[]{:S(2)}, u32[]{:S(2)}) %collective-permute-start.11) | collective-permute-done | bytes 1179680 | tf_op jit(solution)/shard_map/ppermute | solution.py:185
  356.6 1.6 copy-done.8
  358.2 1.4 copy-done.11
  359.6 3.1 update_two.1
  (57 shorter events, 3.3 us)
Async XLA Ops:
  7.2 234.5 %copy-start = (s32[2,1,12,4]{2,3,1,0:T(4,128)S(1)}, s32[2,1,12,4]{2,3,1,0:T(4,128)}, u32[]{:S(2)}) copy-start(s32[2,1,12,4]{2,3,1,0:T(4,128)} %param.13) | copy-start | bytes 1156
  7.2 66.5 %all-gather.6.cloned.1.call-start = ((), (), s32[]{:S(2)}) async-start(), calls=%async_computation | async-start | bytes 5242880 | tf_op jit(solution)/shard_map/all_gather | solution.py:566
  8.2 2.3 copy-start.1
  10.6 1.2 copy-start.12
  13.1 20.7 %collective-permute-start.1 = (bf16[256,1536]{1,0:T(8,128)(2,1)S(1)}, bf16[256,1536]{1,0:T(8,128)(2,1)}, u32[]{:S(2)}, u32[]{:S(2)}) collective-permute-start(bf16[256,1536]{1,0:T(8,128)(2,1)S(1)} %get-tuple-element.24), channel_id=1, source_target_pairs={{0,4},{4,0},{8,12},{12,8},{16,20},{20,16},{24,28},{28,24},{1,5},{5... | collective-permute-start | bytes 2359304 | tf_op jit(solution)/shard_map/ppermute | solution.py:185
  18.3 17.8 %copy-start.17 = (f32[256,1536]{1,0:T(8,128)S(1)}, f32[256,1536]{1,0:T(8,128)}, u32[]{:S(2)}) copy-start(f32[256,1536]{1,0:T(8,128)} %convert_element_type.31) | copy-start | bytes 4718596
  18.3 17.8 %copy-start.18 = (f32[256,512]{1,0:T(8,128)S(1)}, f32[256,512]{1,0:T(8,128)}, u32[]{:S(2)}) copy-start(f32[256,512]{1,0:T(8,128)} %slice.26) | copy-start | bytes 1572868
  36.1 3.3 copy-start.19
  36.1 3.5 copy-start.20
  37.6 168.0 %all-gather.8.cloned.1.call-start = ((), (), s32[]{:S(2)}) async-start(), calls=%async_computation.1 | async-start | bytes 5242880 | tf_op jit(solution)/shard_map/all_gather | solution.py:571
  37.6 78.3 %collective-permute-start = (bf16[3,256,1536]{2,1,0:T(8,128)(2,1)S(1)}, bf16[3,256,1536]{2,1,0:T(8,128)(2,1)}, u32[]{:S(2)}, u32[]{:S(2)}) collective-permute-start(bf16[3,256,1536]{2,1,0:T(8,128)(2,1)S(1)} %get-tuple-element.23.mine_ref), channel_id=1, source_target_pairs={{0,4},{4,0},{8,12},{12,8},{16,20},{20,16},{24,28},{28,24},{1,5},{5... | collective-permute-start | bytes 7077896 | tf_op jit(solution)/shard_map/ppermute | solution.py:185
  73.6 2.2 copy-start.4
  113.9 2.0 copy-start.6
  126.7 1.2 copy-start.9
  127.9 147.0 %all-gather.10.cloned.1.call-start = ((), (), s32[]{:S(2)}) async-start(), calls=%async_computation.2 | async-start | bytes 5242880 | tf_op jit(solution)/shard_map/all_gather | solution.py:584
  128.0 2.3 copy-start.2
  130.3 75.2 %copy-start.10 = (bf16[3,256,1024]{2,1,0:T(8,128)(2,1)S(1)}, bf16[3,256,1024]{2,1,0:T(8,128)(2,1)}, u32[]{:S(2)}) copy-start(bf16[3,256,1024]{2,1,0:T(8,128)(2,1)} %copy-done.9) | copy-start | bytes 4718596
  132.9 1.6 copy-start.7
  134.5 71.0 %collective-permute-start.2 = (bf16[3,256,2048]{2,1,0:T(8,128)(2,1)S(1)}, bf16[3,256,2048]{2,1,0:T(8,128)(2,1)}, u32[]{:S(2)}, u32[]{:S(2)}) collective-permute-start(bf16[3,256,2048]{2,1,0:T(8,128)(2,1)S(1)} %get-tuple-element.29), channel_id=1, source_target_pairs={{0,4},{4,0},{8,12},{12,8},{16,20},{20,16},{24,28},{28,24},{1,5},{5... | collective-permute-start | bytes 9437192 | tf_op jit(solution)/shard_map/ppermute | solution.py:185
  136.0 81.1 %collective-permute-start.4 = (bf16[4,256,256]{2,1,0:T(8,128)(2,1)}, bf16[4,256,256]{2,1,0:T(8,128)(2,1)}, u32[]{:S(2)}, u32[]{:S(2)}) collective-permute-start(bf16[4,256,256]{2,1,0:T(8,128)(2,1)} %bitcast.5), channel_id=1, source_target_pairs={{0,4},{4,0},{8,12},{12,8},{16,20},{20,16},{24,28},{28,24},{1,5},{5... | collective-permute-start | bytes 1572872 | tf_op jit(solution)/shard_map/ppermute | solution.py:185
  215.5 6.0 %copy-start.14 = (bf16[3,256,768]{2,1,0:T(8,128)(2,1)}, bf16[3,256,768]{2,1,0:T(8,128)(2,1)S(1)}, u32[]{:S(2)}) copy-start(bf16[3,256,768]{2,1,0:T(8,128)(2,1)S(1)} %get-tuple-element.40) | copy-start | bytes 3538948
  215.6 6.0 %copy-start.15 = (bf16[3,256,256]{2,1,0:T(8,128)(2,1)}, bf16[3,256,256]{2,1,0:T(8,128)(2,1)S(1)}, u32[]{:S(2)}) copy-start(bf16[3,256,256]{2,1,0:T(8,128)(2,1)S(1)} %get-tuple-element.33) | copy-start | bytes 1179652
  215.6 5.0 %collective-permute-start.8 = (bf16[256,256]{1,0:T(8,128)(2,1)S(1)}, bf16[256,256]{1,0:T(8,128)(2,1)S(1)}, u32[]{:S(2)}, u32[]{:S(2)}) collective-permute-start(bf16[256,256]{1,0:T(8,128)(2,1)S(1)} %get-tuple-element.35), channel_id=1, source_target_pairs={{0,8},{4,12},{8,0},{12,4},{16,24},{20,28},{24,16},{28,20},{1,9},{5... | collective-permute-start | bytes 393224 | tf_op jit(solution)/shard_map/ppermute | solution.py:185
  221.6 6.4 %collective-permute-start.9 = (f32[256,256]{1,0:T(8,128)S(1)}, f32[256,256]{1,0:T(8,128)S(1)}, u32[]{:S(2)}, u32[]{:S(2)}) collective-permute-start(f32[256,256]{1,0:T(8,128)S(1)} %convert_add_fusion), channel_id=1, source_target_pairs={{0,4},{4,0},{8,12},{12,8},{16,20},{20,16},{24,28},{28,24},{1,5},{5... | collective-permute-start | bytes 786440 | tf_op jit(solution)/shard_map/ppermute | solution.py:185
  223.2 16.8 %copy-start.16 = (bf16[3,256,256]{2,1,0:T(8,128)(2,1)S(1)}, bf16[3,256,256]{2,1,0:T(8,128)(2,1)}, u32[]{:S(2)}) copy-start(bf16[3,256,256]{2,1,0:T(8,128)(2,1)} %copy-done.15) | copy-start | bytes 1179652
  228.1 10.7 %collective-permute-start.10 = (f32[256,512]{1,0:T(8,128)S(1)}, f32[256,512]{1,0:T(8,128)S(1)}, u32[]{:S(2)}, u32[]{:S(2)}) collective-permute-start(f32[256,512]{1,0:T(8,128)S(1)} %maximum_select_fusion.2), channel_id=1, source_target_pairs={{0,8},{4,12},{8,0},{12,4},{16,24},{20,28},{24,16},{28,20},{1,9},{5... | collective-permute-start | bytes 1572872 | tf_op jit(solution)/shard_map/ppermute | solution.py:185
  240.0 116.6 %all-gather.12.cloned.1.call-start = ((), (), s32[]{:S(2)}) async-start(), calls=%async_computation.3 | async-start | bytes 2621440 | tf_op jit(solution)/shard_map/all_gather | solution.py:599
  240.0 8.1 %collective-permute-start.3 = (bf16[3,256,256]{2,1,0:T(8,128)(2,1)S(1)}, bf16[3,256,256]{2,1,0:T(8,128)(2,1)S(1)}, u32[]{:S(2)}, u32[]{:S(2)}) collective-permute-start(bf16[3,256,256]{2,1,0:T(8,128)(2,1)S(1)} %copy-done.16), channel_id=1, source_target_pairs={{0,8},{4,12},{8,0},{12,4},{16,24},{20,28},{24,16},{28,20},{1,9},{5... | collective-permute-start | bytes 1179656 | tf_op jit(solution)/shard_map/ppermute | solution.py:185
  249.3 13.8 %collective-permute-start.5 = (f32[768,256]{1,0:T(8,128)S(1)}, f32[768,256]{1,0:T(8,128)S(1)}, u32[]{:S(2)}, u32[]{:S(2)}) collective-permute-start(f32[768,256]{1,0:T(8,128)S(1)} %bitcast.25), channel_id=1, source_target_pairs={{0,4},{4,0},{8,12},{12,8},{16,20},{20,16},{24,28},{28,24},{1,5},{5... | collective-permute-start | bytes 2359304 | tf_op jit(solution)/shard_map/ppermute | solution.py:185
  252.2 65.1 %collective-permute-start.6 = (f32[768,256]{1,0:T(8,128)S(1)}, f32[768,256]{1,0:T(8,128)S(1)}, u32[]{:S(2)}, u32[]{:S(2)}) collective-permute-start(f32[768,256]{1,0:T(8,128)S(1)} %bitcast.26), channel_id=1, source_target_pairs={{0,8},{4,12},{8,0},{12,4},{16,24},{20,28},{24,16},{28,20},{1,9},{5... | collective-permute-start | bytes 2359304 | tf_op jit(solution)/shard_map/ppermute | solution.py:185
  263.2 54.2 %collective-permute-start.7 = (f32[768,256]{1,0:T(8,128)S(1)}, f32[768,256]{1,0:T(8,128)}, u32[]{:S(2)}, u32[]{:S(2)}) collective-permute-start(f32[768,256]{1,0:T(8,128)S(1)} %collective-permute-done.5.x_ref), channel_id=1, source_target_pairs={{0,8},{4,12},{8,0},{12,4},{16,24},{20,28},{24,16},{28,20},{1,9},{5... | collective-permute-start | bytes 2359304 | tf_op jit(solution)/shard_map/ppermute | solution.py:185
  275.0 2.2 copy-start.3
  315.4 2.0 copy-start.5
  327.4 0.8 copy-start.13
  328.2 28.4 %collective-permute-start.11 = (bf16[3,256,768]{2,1,0:T(8,128)(2,1)}, bf16[3,256,768]{2,1,0:T(8,128)(2,1)S(1)}, u32[]{:S(2)}, u32[]{:S(2)}) collective-permute-start(bf16[3,256,768]{2,1,0:T(8,128)(2,1)} %copy-done.14), channel_id=1, source_target_pairs={{0,8},{4,12},{8,0},{12,4},{16,24},{20,28},{24,16},{28,20},{1,9},{5... | collective-permute-start | bytes 3538952 | tf_op jit(solution)/shard_map/ppermute | solution.py:185
  356.6 1.6 copy-start.8
  358.2 1.4 copy-start.11
Sparse Core Ops, SparseCore 0:
  37.7 35.8 all-gather.5
  128.0 34.5 all-gather.7
  240.1 34.8 all-gather.9
  328.3 22.6 all-gather.11
